TPU v7x, 32 devices: a whole 2x2x4 slice. The times are simulated.
32 devices in a mesh: section: 2 (over core), batch: 16 (over z, y, x).
Axes of the slice: x: 2, y: 2, z: 4, core: 2. Of those that a mesh axis runs over, the one named last changes fastest.
Arguments:
- x_query: bfloat16 [128, 32, 768], P('batch'), may hold values from -6 to 6
- x_passage: bfloat16 [32, 256, 768], P('batch'), may hold values from -6 to 6
- len_query: int32 [128], P('batch'), may hold values from 16 to 32, as said below
- len_passage: int32 [32], P('batch'), may hold values from 33 to 256, as said below
- positive: int32 [128], P('batch'), may hold values from 0 to 31
- cot_query: bfloat16 [128, 32, 768], P('batch'), may hold values from -6 to 6
- cot_passage: bfloat16 [32, 256, 768], P('batch'), may hold values from -6 to 6
- w_qkv: bfloat16 [2, 768, 2304], P('section'), may hold values from -0.21875 to 0.21875
- b_qv: float32 [2, 1536], P('section'), may hold values from -3 to 3
- w_o: bfloat16 [2, 768, 768], P('section'), may hold values from -1.75 to 1.75
- b_o: float32 [2, 768], P('section'), may hold values from -3 to 3
- g_attn: float32 [2, 768], P('section'), may hold values from 0.5 to 1.5
- c_attn: float32 [2, 768], P('section'), may hold values from -2 to 2
- w_in: bfloat16 [2, 768, 3072], P('section'), may hold values from -0.21875 to 0.21875
- b_in: float32 [2, 3072], P('section'), may hold values from -3 to 3
- w_out: bfloat16 [2, 3072, 768], P('section'), may hold values from -0.109375 to 0.109375
- b_out: float32 [2, 768], P('section'), may hold values from -3 to 3
- g_ffn: float32 [2, 768], P('section'), may hold values from 0.5 to 1.5
- c_ffn: float32 [2, 768], P('section'), may hold values from -2 to 2
Outputs:
- hidden_query: bfloat16 [2, 128, 32, 768], P('section', 'batch')
- hidden_passage: bfloat16 [2, 32, 256, 768], P('section', 'batch')
- grad_query: float32 [2, 128, 32, 768], P('section', 'batch')
- grad_passage: float32 [2, 32, 256, 768], P('section', 'batch')
- loss_value: float32 [], replicated
- d_w_qkv: float32 [2, 768, 2304], P('section', 'batch')
- d_b_qv: float32 [2, 1536], P('section', 'batch')
- d_w_o: float32 [2, 768, 768], P('section', 'batch')
- d_b_o: float32 [2, 768], P('section', 'batch')
- d_g_attn: float32 [2, 768], P('section', 'batch')
- d_c_attn: float32 [2, 768], P('section', 'batch')
- d_w_in: float32 [2, 768, 3072], P('section', 'batch')
- d_b_in: float32 [2, 3072], P('section', 'batch')
- d_w_out: float32 [2, 3072, 768], P('section', 'batch')
- d_b_out: float32 [2, 768], P('section', 'batch')
- d_g_ffn: float32 [2, 768], P('section', 'batch')
- d_c_ffn: float32 [2, 768], P('section', 'batch')
Inputs may be any that keep to these rules, and one draw needn't show every extreme that they name: `len_query`: valid tokens of each query, from the start of its 32 slots; some query has exactly 32. `len_passage`: valid tokens of each passage, from the start of its 256 slots; most are short, some fill all 256; some passage has exactly 256.
All inputs are finite; a program needn't handle non-finite values.
Results may differ from a plain program's by a relative error of at most 0.028.
Values may be sent and summed in bfloat16 or wider, within the bound.
A program may use at most 256 MiB of HBM per device.

v0:
```python
import math

import jax
import jax.numpy as jnp
from jax import lax
from jax.sharding import PartitionSpec as P

HEADS = 12
QLEN = 32
PLEN = 256
MICRO = 2


norm_eps = 1e-05


def shifted(value, axis, steps):
    count = lax.axis_size(axis)
    first, last = (max(0, -steps), min(count, count - steps))
    return lax.ppermute(value, axis, [(source, source + steps) for source in range(first, last)])


def normalize(inputs, gain_vec, shift_vec):
    mean_val = jnp.mean(inputs, -1, keepdims=True)
    centred = inputs - mean_val
    spread = jnp.mean(centred * centred, -1, keepdims=True)
    return centred * lax.rsqrt(spread + norm_eps) * gain_vec + shift_vec


def exact_gelu(inputs):
    return jax.nn.gelu(inputs, approximate=False)


def head_split(rows, seq_count, length):
    return rows.reshape(seq_count, length, HEADS, rows.shape[1] // HEADS)


def masked_scores(q_heads, k_heads, lengths, length):
    head_size = q_heads.shape[3]
    scores = jnp.einsum(
        "sqhd,skhd->shqk", q_heads, k_heads, preferred_element_type=jnp.float32
    ) * head_size ** (-0.5)
    valid_mask = jnp.arange(length)[None, :] < lengths[:, None]
    return jnp.where(valid_mask[:, None, None, :], scores, -1000000000.0)


def attend_forward(queries, key_rows, values, lengths, length):
    seq_count = lengths.shape[0]
    q_heads = head_split(queries, seq_count, length)
    k_heads = head_split(key_rows, seq_count, length)
    v_heads = head_split(values, seq_count, length)
    scores = masked_scores(q_heads, k_heads, lengths, length)
    top_score = jnp.max(scores, -1, keepdims=True)
    weights = jnp.exp(scores - top_score)
    total_sum = jnp.sum(weights, -1, keepdims=True)
    probs_low = (weights / total_sum).astype(jnp.bfloat16)
    mixed = jnp.einsum("shqk,skhd->sqhd", probs_low, v_heads, preferred_element_type=jnp.float32)
    return (mixed.reshape(queries.shape).astype(jnp.bfloat16), top_score + jnp.log(total_sum))


def attend_backward(queries, key_rows, values, lengths, length, log_sums, grad_mixed):
    seq_count = lengths.shape[0]
    q_heads = head_split(queries, seq_count, length)
    k_heads = head_split(key_rows, seq_count, length)
    v_heads = head_split(values, seq_count, length)
    head_scale = q_heads.shape[3] ** (-0.5)
    probs_full = jnp.exp(masked_scores(q_heads, k_heads, lengths, length) - log_sums)
    grad_heads = head_split(grad_mixed, seq_count, length)
    grad_probs = jnp.einsum(
        "sqhd,skhd->shqk", grad_heads, v_heads, preferred_element_type=jnp.float32
    )
    grad_values = jnp.einsum(
        "shqk,sqhd->skhd",
        probs_full.astype(jnp.bfloat16),
        grad_heads,
        preferred_element_type=jnp.float32,
    )
    inner_sum = jnp.sum(grad_probs * probs_full, -1, keepdims=True)
    grad_scores = (probs_full * (grad_probs - inner_sum)).astype(jnp.bfloat16)
    grad_queries = (
        jnp.einsum("shqk,skhd->sqhd", grad_scores, k_heads, preferred_element_type=jnp.float32)
        * head_scale
    )
    grad_keys = (
        jnp.einsum("shqk,sqhd->skhd", grad_scores, q_heads, preferred_element_type=jnp.float32)
        * head_scale
    )
    return tuple(
        (
            member.reshape(queries.shape).astype(jnp.bfloat16)
            for member in (grad_queries, grad_keys, grad_values)
        )
    )


def layer_forward(token_rows, query_lens, passage_lens, params):
    w_qkv, b_qv, w_o, b_o, g_attn, c_attn, w_in, b_in, w_out, b_out, g_ffn, c_ffn = params
    features = token_rows.shape[1]
    projected = jnp.dot(token_rows, w_qkv, preferred_element_type=jnp.float32)
    queries = (projected[:, :features] + b_qv[:features]).astype(jnp.bfloat16)
    key_rows = projected[:, features : 2 * features].astype(jnp.bfloat16)
    values = (projected[:, 2 * features :] + b_qv[features:]).astype(jnp.bfloat16)
    query_rows = query_lens.shape[0] * QLEN
    mixed_q, sums_q = attend_forward(
        queries[:query_rows], key_rows[:query_rows], values[:query_rows], query_lens, QLEN
    )
    mixed_p, sums_p = attend_forward(
        queries[query_rows:], key_rows[query_rows:], values[query_rows:], passage_lens, PLEN
    )
    mixed_rows = jnp.concatenate([mixed_q, mixed_p], 0)
    pre_attn = (
        token_rows.astype(jnp.float32)
        + jnp.dot(mixed_rows, w_o, preferred_element_type=jnp.float32)
        + b_o
    )
    normed = normalize(pre_attn, g_attn, c_attn)
    normed_low = normed.astype(jnp.bfloat16)
    up_proj = jnp.dot(normed_low, w_in, preferred_element_type=jnp.float32) + b_in
    act_low = exact_gelu(up_proj).astype(jnp.bfloat16)
    pre_ffn = normed + jnp.dot(act_low, w_out, preferred_element_type=jnp.float32) + b_out
    kept_state = (
        token_rows,
        queries,
        key_rows,
        values,
        mixed_rows,
        sums_q,
        sums_p,
        pre_attn,
        normed_low,
        up_proj,
        act_low,
        pre_ffn,
        query_lens,
        passage_lens,
    )
    return (normalize(pre_ffn, g_ffn, c_ffn), kept_state)


def layer_backward(kept_state, params, grad_out):
    (
        token_rows,
        queries,
        key_rows,
        values,
        mixed_rows,
        sums_q,
        sums_p,
        pre_attn,
        normed_low,
        up_proj,
        act_low,
        pre_ffn,
        query_lens,
        passage_lens,
    ) = kept_state
    w_qkv, b_qv, w_o, b_o, g_attn, c_attn, w_in, b_in, w_out, b_out, g_ffn, c_ffn = params
    unused, ffn_norm_back = jax.vjp(normalize, pre_ffn, g_ffn, c_ffn)
    grad_pre_ffn, grad_g_ffn, grad_c_ffn = ffn_norm_back(grad_out)
    grad_ffn_low = grad_pre_ffn.astype(jnp.bfloat16)
    grad_b_out = jnp.sum(grad_pre_ffn, 0)
    grad_w_out = jnp.einsum("rf,rd->fd", act_low, grad_ffn_low, preferred_element_type=jnp.float32)
    grad_act = jnp.einsum("rd,fd->rf", grad_ffn_low, w_out, preferred_element_type=jnp.float32)
    unused, gelu_back = jax.vjp(exact_gelu, up_proj)
    grad_up = gelu_back(grad_act)[0].astype(jnp.bfloat16)
    grad_b_in = jnp.sum(grad_up.astype(jnp.float32), 0)
    grad_w_in = jnp.einsum("rd,rf->df", normed_low, grad_up, preferred_element_type=jnp.float32)
    grad_normed = grad_pre_ffn + jnp.einsum(
        "rf,df->rd", grad_up, w_in, preferred_element_type=jnp.float32
    )
    unused, attn_norm_back = jax.vjp(normalize, pre_attn, g_attn, c_attn)
    grad_pre_attn, grad_g_attn, grad_c_attn = attn_norm_back(grad_normed)
    grad_attn_low = grad_pre_attn.astype(jnp.bfloat16)
    grad_b_o = jnp.sum(grad_pre_attn, 0)
    grad_w_o = jnp.einsum(
        "re,rd->ed", mixed_rows, grad_attn_low, preferred_element_type=jnp.float32
    )
    grad_mixed = jnp.einsum(
        "rd,ed->re", grad_attn_low, w_o, preferred_element_type=jnp.float32
    ).astype(jnp.bfloat16)
    query_rows = query_lens.shape[0] * QLEN
    grads_q = attend_backward(
        queries[:query_rows],
        key_rows[:query_rows],
        values[:query_rows],
        query_lens,
        QLEN,
        sums_q,
        grad_mixed[:query_rows],
    )
    grads_p = attend_backward(
        queries[query_rows:],
        key_rows[query_rows:],
        values[query_rows:],
        passage_lens,
        PLEN,
        sums_p,
        grad_mixed[query_rows:],
    )
    stacked = tuple((jnp.concatenate([left, right], 0) for left, right in zip(grads_q, grads_p)))
    grad_proj = jnp.concatenate(stacked, 1)
    grad_b_qv = jnp.concatenate(
        [jnp.sum(stacked[0].astype(jnp.float32), 0), jnp.sum(stacked[2].astype(jnp.float32), 0)]
    )
    grad_w_qkv = jnp.einsum("rd,re->de", token_rows, grad_proj, preferred_element_type=jnp.float32)
    grad_rows = grad_pre_attn + jnp.einsum(
        "re,de->rd", grad_proj, w_qkv, preferred_element_type=jnp.float32
    )
    return (
        grad_rows,
        (
            grad_w_qkv,
            grad_b_qv,
            grad_w_o,
            grad_b_o,
            grad_g_attn,
            grad_c_attn,
            grad_w_in,
            grad_b_in,
            grad_w_out,
            grad_b_out,
            grad_g_ffn,
            grad_c_ffn,
        ),
    )


def contrast(logits, targets):
    top_score = jnp.max(logits, -1, keepdims=True)
    log_total = top_score[:, 0] + jnp.log(jnp.sum(jnp.exp(logits - top_score), -1))
    chosen = targets[:, None] == jnp.arange(logits.shape[1])[None, :]
    term_values = log_total - jnp.sum(jnp.where(chosen, logits, 0.0), -1)
    grad_logits = (jnp.exp(logits - log_total[:, None]) - chosen.astype(jnp.float32)).astype(
        jnp.bfloat16
    )
    return (term_values, grad_logits)


def take_block(array, block_index, block_size):
    return array[block_index * block_size : (block_index + 1) * block_size]


def per_device(
    x_query,
    x_passage,
    len_query,
    len_passage,
    positive,
    cot_query,
    cot_passage,
    w_qkv,
    b_qv,
    w_o,
    b_o,
    g_attn,
    c_attn,
    w_in,
    b_in,
    w_out,
    b_out,
    g_ffn,
    c_ffn,
):
    params = tuple(
        (
            member[0]
            for member in (
                w_qkv,
                b_qv,
                w_o,
                b_o,
                g_attn,
                c_attn,
                w_in,
                b_in,
                w_out,
                b_out,
                g_ffn,
                c_ffn,
            )
        )
    )
    on_first = lax.axis_index("section") == 0
    query_per = x_query.shape[0] // MICRO
    passage_per = x_passage.shape[0] // MICRO
    features = x_query.shape[2]
    query_rows = query_per * QLEN
    received = jnp.zeros((query_rows + passage_per * PLEN, features), jnp.bfloat16)
    stored = []
    outputs = []
    for moment in range(MICRO + 1):
        early_mb = min(moment, MICRO - 1)
        late_mb = max(moment - 1, 0)
        rows_in = jnp.where(
            on_first,
            jnp.concatenate(
                [
                    take_block(x_query, early_mb, query_per).reshape(-1, features),
                    take_block(x_passage, early_mb, passage_per).reshape(-1, features),
                ],
                0,
            ),
            received,
        )
        query_lens = jnp.where(
            on_first,
            take_block(len_query, early_mb, query_per),
            take_block(len_query, late_mb, query_per),
        )
        passage_lens = jnp.where(
            on_first,
            take_block(len_passage, early_mb, passage_per),
            take_block(len_passage, late_mb, passage_per),
        )
        result, kept_state = layer_forward(rows_in, query_lens, passage_lens, params)
        result_low = result.astype(jnp.bfloat16)
        outputs.append(result_low)
        stored.append(kept_state)
        if moment < MICRO:
            received = shifted(result_low, "section", 1)
    finals = [
        jnp.where(on_first, outputs[block_index], outputs[block_index + 1])
        for block_index in range(MICRO)
    ]
    hidden_q = jnp.concatenate(
        [final[:query_rows].reshape(query_per, QLEN, features) for final in finals], 0
    )
    hidden_p = jnp.concatenate(
        [final[query_rows:].reshape(passage_per, PLEN, features) for final in finals], 0
    )
    cls_query = hidden_q[:, 0]
    cls_passage = hidden_p[:, 0]
    score_scale = 2.0 / math.sqrt(features)
    own_queries = x_query.shape[0]
    gathered = lax.all_gather(cls_passage, "batch", axis=0, tiled=True)
    logits = (
        jnp.einsum("qd,pd->qp", cls_query, gathered, preferred_element_type=jnp.float32)
        * score_scale
    )
    term_values, grad_logits = contrast(logits, positive)
    grad_cls_q = (
        jnp.einsum("qp,pd->qd", grad_logits, gathered, preferred_element_type=jnp.float32)
        * score_scale
    )
    passage_terms = (
        jnp.einsum("qp,qd->pd", grad_logits, cls_query, preferred_element_type=jnp.float32)
        * score_scale
    )
    grad_cls_p = lax.psum_scatter(passage_terms, "batch", scatter_dimension=0, tiled=True)
    summed_loss = lax.psum(jnp.where(on_first, 0.0, jnp.sum(term_values)), ("section", "batch"))
    loss_value = summed_loss / (own_queries * lax.axis_size("batch"))
    back_grad = jnp.zeros_like(received)
    grad_totals = None
    row_grads = []
    for moment in range(MICRO + 1):
        upper_mb = min(moment, MICRO - 1)
        lower_mb = max(moment - 1, 0)
        rows_list = []
        for cot_block, lens_block, cls_grad, length, block_size in (
            (cot_query, len_query, grad_cls_q, QLEN, query_per),
            (cot_passage, len_passage, grad_cls_p, PLEN, passage_per),
        ):
            valid_mask = (
                jnp.arange(length)[None, :] < take_block(lens_block, upper_mb, block_size)[:, None]
            )
            masked = jnp.where(
                valid_mask[:, :, None],
                take_block(cot_block, upper_mb, block_size).astype(jnp.float32),
                0.0,
            )
            head_rows = jnp.concatenate(
                [
                    take_block(cls_grad, upper_mb, block_size)[:, None, :],
                    jnp.zeros((block_size, length - 1, features), jnp.float32),
                ],
                1,
            )
            rows_list.append((masked + head_rows).reshape(block_size * length, features))
        grad_in = jnp.where(on_first, back_grad.astype(jnp.float32), jnp.concatenate(rows_list, 0))
        active = jnp.where(on_first, moment >= 1, moment < MICRO)
        saved_state = jax.tree.map(
            lambda left, right: jnp.where(on_first, left, right),
            stored[lower_mb],
            stored[upper_mb + 1],
        )
        kept_state = saved_state
        grad_rows, grad_set = layer_backward(kept_state, params, grad_in)
        grad_set = jax.tree.map(lambda grad_item: jnp.where(active, grad_item, 0.0), grad_set)
        if grad_totals is None:
            grad_totals = tuple(grad_set)
        else:
            grad_totals = tuple((left + right for left, right in zip(grad_totals, grad_set)))
        row_grads.append(grad_rows)
        if moment < MICRO:
            back_grad = shifted(grad_rows.astype(jnp.bfloat16), "section", -1)
    grad_finals = [
        jnp.where(on_first, row_grads[block_index + 1], row_grads[block_index])
        for block_index in range(MICRO)
    ]
    grad_q = jnp.concatenate(
        [final[:query_rows].reshape(query_per, QLEN, features) for final in grad_finals], 0
    )
    grad_p = jnp.concatenate(
        [final[query_rows:].reshape(passage_per, PLEN, features) for final in grad_finals], 0
    )
    summed = (
        lax.psum_scatter(grad_totals[0], "batch", scatter_dimension=0, tiled=True),
        lax.psum_scatter(grad_totals[1], "batch", scatter_dimension=0, tiled=True),
        lax.psum_scatter(grad_totals[2], "batch", scatter_dimension=0, tiled=True),
        lax.psum_scatter(grad_totals[3], "batch", scatter_dimension=0, tiled=True),
        lax.psum_scatter(grad_totals[4], "batch", scatter_dimension=0, tiled=True),
        lax.psum_scatter(grad_totals[5], "batch", scatter_dimension=0, tiled=True),
        lax.psum_scatter(grad_totals[6], "batch", scatter_dimension=0, tiled=True),
        lax.psum_scatter(grad_totals[7], "batch", scatter_dimension=0, tiled=True),
        lax.psum_scatter(grad_totals[8], "batch", scatter_dimension=0, tiled=True),
        lax.psum_scatter(grad_totals[9], "batch", scatter_dimension=0, tiled=True),
        lax.psum_scatter(grad_totals[10], "batch", scatter_dimension=0, tiled=True),
        lax.psum_scatter(grad_totals[11], "batch", scatter_dimension=0, tiled=True),
    )
    return (
        hidden_q[None],
        hidden_p[None],
        grad_q[None],
        grad_p[None],
        loss_value,
        summed[0][None],
        summed[1][None],
        summed[2][None],
        summed[3][None],
        summed[4][None],
        summed[5][None],
        summed[6][None],
        summed[7][None],
        summed[8][None],
        summed[9][None],
        summed[10][None],
        summed[11][None],
    )


def solution(mesh):
    in_specs = (
        P("batch", None, None),
        P("batch", None, None),
        P("batch"),
        P("batch"),
        P("batch"),
        P("batch", None, None),
        P("batch", None, None),
        P("section", None, None),
        P("section", None),
        P("section", None, None),
        P("section", None),
        P("section", None),
        P("section", None),
        P("section", None, None),
        P("section", None),
        P("section", None, None),
        P("section", None),
        P("section", None),
        P("section", None),
    )
    out_specs = (
        P("section", "batch", None, None),
        P("section", "batch", None, None),
        P("section", "batch", None, None),
        P("section", "batch", None, None),
        P(),
        P("section", "batch", None),
        P("section", "batch"),
        P("section", "batch", None),
        P("section", "batch"),
        P("section", "batch"),
        P("section", "batch"),
        P("section", "batch", None),
        P("section", "batch"),
        P("section", "batch", None),
        P("section", "batch"),
        P("section", "batch"),
        P("section", "batch"),
    )
    return jax.shard_map(
        per_device, mesh=mesh, in_specs=in_specs, out_specs=out_specs, check_vma=False
    )
```

profile of v0, /device:TPU:0, one launch (start us, length us, event | category | flops | bytes accessed | tf_op | source)
XLA Modules:
  0.0 1222.9 jit_solution(17208940515153888525)
XLA Ops:
  52.7 15.1 %fusion.2 = (bf16[384,3072]{1,0:T(8,128)(2,1)S(1)}, f32[384,3072]{1,0:T(8,128)}) fusion(f32[3072]{0:T(1024)S(1)} %bitcast.489, bf16[1,768,3072]{2,1,0:T(8,128)(2,1)} %param.32, f32[384,768]{1,0:T(8,128)S(1)} %get-tuple-element.171, f32[768]{0:T(1024)S(1)} %reduce.22, f32[768]{0:T(1024)S(1)} %reduce.21, f32[384]{0:T(512)S(1)} %add_rsqrt_fusion.5, ...), kind=kOutput, calls=%fused_computation.11 | convolution fusion | flops 1891270656 | bytes 12997632 | tf_op jit(solution)/shard_map/dot_general | solution.py:118
  126.8 15.1 %fusion.5 = (bf16[384,3072]{1,0:T(8,128)(2,1)S(1)}, f32[384,3072]{1,0:T(8,128)}) fusion(f32[3072]{0:T(1024)S(1)} %bitcast.490, bf16[1,768,3072]{2,1,0:T(8,128)(2,1)} %param.32, f32[384,768]{1,0:T(8,128)S(1)} %get-tuple-element.183, f32[384]{0:T(512)S(1)} %add_rsqrt_fusion.3, f32[384]{0:T(512)S(1)} %broadcast_multiply_fusion.9, f32[768]{0:T(1024)S(1)} %reduce.22, ...), kind=kOutput, calls=%fused_computation.14 | convolution fusion | flops 1891270656 | bytes 12997632 | tf_op jit(solution)/shard_map/dot_general | solution.py:118
  202.0 14.8 %fusion.8 = (bf16[384,3072]{1,0:T(8,128)(2,1)S(1)}, f32[384,3072]{1,0:T(8,128)}) fusion(f32[3072]{0:T(1024)S(1)} %bitcast.491, bf16[384,768]{1,0:T(8,128)(2,1)S(1)} %get-tuple-element.128, bf16[1,768,3072]{2,1,0:T(8,128)(2,1)} %param.32), kind=kOutput, calls=%fused_computation.17 | convolution fusion | flops 1889796096 | bytes 12398592 | tf_op jit(solution)/shard_map/dot_general | solution.py:118
  224.4 42.3 %all-gather = bf16[32,1,768]{2,1,0:T(2,128)(2,1)S(1)} all-gather(bf16[2,1,768]{2,1,0:T(2,128)(2,1)S(1)} %fusion.325), channel_id=2, replica_groups=mesh['section'=2,'batch'=16] {'batch'}, dimensions={0}, use_global_device_ids=true | all-gather | bytes 52224 | tf_op jit(solution)/shard_map/all_gather | solution.py:335
  322.3 59.8 %all-reduce.16.cloned.1.call-done = f32[32,768]{1,0:T(8,128)} async-done(((f32[32,768]{1,0:T(8,128)}), f32[32,768]{1,0:T(8,128)}) %all-reduce.16.cloned.1.call-update) | async-done | bytes 98320
  389.4 16.0 %convert_reduce_fusion.2 = (f32[3072]{0:T(1024)}, bf16[384,3072]{1,0:T(8,128)(2,1)S(1)}) fusion(bf16[1,3072,768]{2,1,0:T(8,128)(2,1)} %param.34, f32[384,768]{1,0:T(8,128)S(1)} %get-tuple-element.110, f32[384]{0:T(512)S(1)} %negate_multiply_fusion.11, f32[384,3072]{1,0:T(8,128)} %get-tuple-element.173, f32[384,3072]{1,0:T(8,128)} %get-tuple-element.185, ...), kind=kOutput, calls=%fused_computation.59 | convolution fusion | flops 1900999680 | bytes 17708544 | tf_op jit(solution)/shard_map/rd,fd->rf/dot_general | solution.py:163
  443.9 4.8 fusion.386
  473.9 3.7 subtract_exponential_fusion
  481.8 16.2 %convert_reduce_fusion.1 = (f32[3072]{0:T(1024)}, bf16[384,3072]{1,0:T(8,128)(2,1)S(1)}) fusion(bf16[1,3072,768]{2,1,0:T(8,128)(2,1)} %param.34, f32[384,768]{1,0:T(8,128)S(1)} %get-tuple-element.100, f32[384]{0:T(512)S(1)} %negate_multiply_fusion.9, f32[384,3072]{1,0:T(8,128)} %get-tuple-element.173, f32[384,3072]{1,0:T(8,128)} %get-tuple-element.197, pred[]{:T(512)} %eq.16), kind=kOutput, calls=%fused_computation.58 | convolution fusion | flops 1900999680 | bytes 17708544 | tf_op jit(solution)/shard_map/rd,fd->rf/dot_general | solution.py:163
  536.4 5.2 broadcast_select_fusion.5
  544.3 6.5 fusion.257
  552.7 14.6 %convert_reduce_fusion = (f32[3072]{0:T(1024)}, bf16[384,3072]{1,0:T(8,128)(2,1)S(1)}) fusion(bf16[1,3072,768]{2,1,0:T(8,128)(2,1)S(1)} %bitcast.478, f32[384,768]{1,0:T(8,128)S(1)} %get-tuple-element.92, f32[384]{0:T(512)S(1)} %negate_multiply_fusion.7, f32[384,3072]{1,0:T(8,128)S(1)} %bitcast.495, f32[384,3072]{1,0:T(8,128)S(1)} %bitcast.493, pred[]{:T(512)} %eq.16), kind=kOutput, calls=%fused_computation.57 | convolution fusion | flops 1900999680 | bytes 17708544 | tf_op jit(solution)/shard_map/rd,fd->rf/dot_general | solution.py:163
  575.3 6.7 fusion.255
  620.0 6.8 select_add_fusion.2
  627.5 5.5 fusion.247
  635.9 9.8 select_add_fusion.1
  646.4 4.8 fusion.120
  651.3 5.2 fusion.118
  656.4 8.0 select_add_fusion
  667.1 41.8 %psum.7 = f32[]{:T(128)} all-reduce(f32[]{:T(128)S(6)} %select_n.583), channel_id=1, replica_groups=mesh['section'=2,'batch'=16] {'section','batch'}, use_global_device_ids=true, to_apply=%region_59.60 | all-reduce | flops 1 | bytes 8 | tf_op jit(solution)/shard_map/psum | solution.py:350
  726.6 78.2 %all-reduce.13 = (f32[1536]{0:T(1024)}, f32[768]{0:T(1024)}, f32[768]{0:T(1024)}, f32[768]{0:T(1024)}, f32[3072]{0:T(1024)}, /*index=5*/f32[768]{0:T(1024)}, f32[768]{0:T(1024)}, f32[768]{0:T(1024)}) all-reduce(f32[1536]{0:T(1024)} %fusion.324, ...), channel_id=5, replica_groups=mesh['section'=2,'batch'=16] {'batch'}, use_global_device_ids=true, to_apply=%region_67.68.clone | all-reduce | flops 9216 | bytes 73728
  819.7 42.5 %reduce-scatter.5.cloned.1.call-done = f32[48,2304]{1,0:T(8,128)} async-done(((f32[768,2304]{1,0:T(8,128)}), f32[48,2304]{1,0:T(8,128)}) %reduce-scatter.5.cloned.1.call-update) | async-done | bytes 442384 | tf_op jit(solution)/shard_map/reduce_scatter | solution.py:407
  862.2 176.8 %reduce-scatter.9.cloned.1.call-done = f32[48,3072]{1,0:T(8,128)} async-done(((f32[768,3072]{1,0:T(8,128)}), f32[48,3072]{1,0:T(8,128)}) %reduce-scatter.9.cloned.1.call-update) | async-done | bytes 589840 | tf_op jit(solution)/shard_map/reduce_scatter | solution.py:413
  1039.0 176.1 %reduce-scatter.11.cloned.1.call-done = f32[192,768]{1,0:T(8,128)} async-done(((f32[3072,768]{1,0:T(8,128)}), f32[192,768]{1,0:T(8,128)}) %reduce-scatter.11.cloned.1.call-update) | async-done | bytes 589840 | tf_op jit(solution)/shard_map/reduce_scatter | solution.py:415
  (969 shorter events, 420.4 us)
Async XLA Ops:
  7.2 374.9 %all-reduce.16.cloned.1.call-start = ((), (), s32[]{:S(2)}) async-start(), calls=%async_computation.8 | async-start | bytes 196608
  49.1 167.7 %copy-start.146 = (f32[768]{0:T(1024)}, f32[768]{0:T(1024)S(1)}, u32[]{:S(2)}) copy-start(f32[768]{0:T(1024)S(1)} %reduce.22) | copy-start | bytes 9220
  49.9 18.0 %slice-start.4 = ((s8[4718592]{0:T(1024)(128)(4,1)}), s8[4194304]{0:T(1024)(128)(4,1)S(1)}, s32[]{:S(2)}) async-start(s8[4718592]{0:T(1024)(128)(4,1)} %bitcast.471), calls=%async_computation.13 | async-start | bytes 8388608
  72.2 18.1 %collective-permute-start = (bf16[384,768]{1,0:T(8,128)(2,1)}, bf16[384,768]{1,0:T(8,128)(2,1)}, u32[]{:S(2)}, u32[]{:S(2)}) collective-permute-start(bf16[384,768]{1,0:T(8,128)(2,1)} %add_convert_fusion.2), channel_id=1, source_target_pairs={{0,16},{1,17},{2,18},{3,19},{4,20},{5,21},{6,22},{7,23},{8,24},{9,... | collective-permute-start | bytes 1769480 | tf_op jit(solution)/shard_map/ppermute | solution.py:20
  123.9 17.9 %slice-start.6 = ((s8[4718592]{0:T(1024)(128)(4,1)}), s8[4194304]{0:T(1024)(128)(4,1)S(1)}, s32[]{:S(2)}) async-start(s8[4718592]{0:T(1024)(128)(4,1)} %bitcast.473), calls=%async_computation.15 | async-start | bytes 8388608
  145.7 17.2 %collective-permute-start.1 = (bf16[384,768]{1,0:T(8,128)(2,1)}, bf16[384,768]{1,0:T(8,128)(2,1)}, u32[]{:S(2)}, u32[]{:S(2)}) collective-permute-start(bf16[384,768]{1,0:T(8,128)(2,1)} %get-tuple-element.116), channel_id=1, source_target_pairs={{0,16},{1,17},{2,18},{3,19},{4,20},{5,21},{6,22},{7,23},{8,24},{9,... | collective-permute-start | bytes 1769480 | tf_op jit(solution)/shard_map/ppermute | solution.py:20
  199.2 17.6 %slice-start.8 = ((s8[4718592]{0:T(1024)(128)(4,1)}), s8[4194304]{0:T(1024)(128)(4,1)S(1)}, s32[]{:S(2)}) async-start(s8[4718592]{0:T(1024)(128)(4,1)} %bitcast.475), calls=%async_computation.17 | async-start | bytes 8388608
  222.1 45.2 %copy-start.88 = (bf16[4,32,768]{2,0,1:T(4,128)(2,1)S(1)}, bf16[4,32,768]{2,0,1:T(4,128)(2,1)}, u32[]{:S(2)}) copy-start(bf16[4,32,768]{2,0,1:T(4,128)(2,1)} %copy.258) | copy-start | bytes 589828
  222.1 45.4 %copy-start.267 = (s32[8]{0:T(128)S(1)}, s32[8]{0:T(128)}, u32[]{:S(2)}) copy-start(s32[8]{0:T(128)} %param.23) | copy-start | bytes 100
  223.9 44.6 %copy-start.89 = (bf16[4,32,768]{2,0,1:T(4,128)(2,1)}, bf16[4,32,768]{2,0,1:T(4,128)(2,1)S(1)}, u32[]{:S(2)}) copy-start(bf16[4,32,768]{2,0,1:T(4,128)(2,1)S(1)} %copy.259) | copy-start | bytes 589828
  281.5 16.4 %copy-start.195 = (f32[384]{0:T(512)}, f32[384]{0:T(512)S(1)}, u32[]{:S(2)}) copy-start(f32[384]{0:T(512)S(1)} %broadcast_multiply_fusion.5) | copy-start | bytes 4612
  282.9 536.7 %reduce-scatter.7.cloned.1.call-start = ((), (), s32[]{:S(2)}) async-start(), calls=%async_computation.5 | async-start | bytes 2506752 | tf_op jit(solution)/shard_map/reduce_scatter | solution.py:409
  385.2 20.2 %slice-start.12 = ((s8[4718592]{0:T(1024)(128)(4,1)}), s8[4194304]{0:T(1024)(128)(4,1)S(1)}, s32[]{:S(2)}) async-start(s8[4718592]{0:T(1024)(128)(4,1)} %bitcast.479), calls=%async_computation.21 | async-start | bytes 8388608
  448.6 29.0 %collective-permute-start.2 = (bf16[384,768]{1,0:T(8,128)(2,1)}, bf16[384,768]{1,0:T(8,128)(2,1)}, u32[]{:S(2)}, u32[]{:S(2)}) collective-permute-start(bf16[384,768]{1,0:T(8,128)(2,1)} %get-tuple-element.207), channel_id=1, source_target_pairs={{16,0},{17,1},{18,2},{19,3},{20,4},{21,5},{22,6},{23,7},{24,8},{25... | collective-permute-start | bytes 1769480 | tf_op jit(solution)/shard_map/ppermute | solution.py:20
  477.6 20.3 %slice-start.14 = ((s8[4718592]{0:T(1024)(128)(4,1)}), s8[4194304]{0:T(1024)(128)(4,1)S(1)}, s32[]{:S(2)}) async-start(s8[4718592]{0:T(1024)(128)(4,1)} %bitcast.481), calls=%async_computation.23 | async-start | bytes 8388608
  481.7 16.2 %copy-start.26 = (f32[384,768]{1,0:T(8,128)}, f32[384,768]{1,0:T(8,128)S(1)}, u32[]{:S(2)}) copy-start(f32[384,768]{1,0:T(8,128)S(1)} %get-tuple-element.100) | copy-start | bytes 3538948
  481.7 16.2 %copy-start.207 = (f32[384]{0:T(512)}, f32[384]{0:T(512)S(1)}, u32[]{:S(2)}) copy-start(f32[384]{0:T(512)S(1)} %negate_multiply_fusion.9) | copy-start | bytes 4612
  501.5 71.3 %copy-start.230 = (f32[384]{0:T(512)}, f32[384]{0:T(512)S(1)}, u32[]{:S(2)}) copy-start(f32[384]{0:T(512)S(1)} %negate_multiply_fusion.8) | copy-start | bytes 4612
  541.6 9.3 collective-permute-start.3
  550.9 16.4 %slice-start.16 = ((s8[4718592]{0:T(1024)(128)(4,1)}), s8[4194304]{0:T(1024)(128)(4,1)S(1)}, s32[]{:S(2)}) async-start(s8[4718592]{0:T(1024)(128)(4,1)} %bitcast.483), calls=%async_computation.25 | async-start | bytes 8388608
  575.3 286.9 %reduce-scatter.5.cloned.1.call-start = ((), (), s32[]{:S(2)}) async-start(), calls=%async_computation.4 | async-start | bytes 7520256 | tf_op jit(solution)/shard_map/reduce_scatter | solution.py:407
  626.8 412.2 %reduce-scatter.9.cloned.1.call-start = ((), (), s32[]{:S(2)}) async-start(), calls=%async_computation.6 | async-start | bytes 10027008 | tf_op jit(solution)/shard_map/reduce_scatter | solution.py:413
  645.7 569.4 %reduce-scatter.11.cloned.1.call-start = ((), (), s32[]{:S(2)}) async-start(), calls=%async_computation.7 | async-start | bytes 10027008 | tf_op jit(solution)/shard_map/reduce_scatter | solution.py:415
  664.5 52.0 %copy-start.204 = (f32[384]{0:T(512)S(1)}, f32[384]{0:T(512)}, u32[]{:S(2)}) copy-start(f32[384]{0:T(512)} %copy-done.202) | copy-start | bytes 4612
  (287 other events, 1487.3 us)
Sparse Core Ops, SparseCore 0:
  283.1 99.0 all-reduce.15
  575.4 130.1 reduce-scatter.6
  712.3 149.8 reduce-scatter.4
  869.3 169.7 reduce-scatter.8
  1045.1 169.9 reduce-scatter.10
where the time goes:
time: 1230 us; the launch traced here: 1220 us
  waiting for transfers between devices  455 us (37%)
  matrix products  270 us (22%)
  local copies, waits for them, and re-layouts  217 us (18%)
  blocking collectives  162 us (13%)
  other arithmetic  83.1 us (7%)
  between operations  26.3 us (2%)
    reduce_scatter x1, waiting for transfers between devices, per_device(): lax.psum_scatter(grad_totals[6], 'batch', scatter_dimension=0, tiled=True)  177 us
    reduce_scatter x1, waiting for transfers between devices, per_device(): lax.psum_scatter(grad_totals[8], 'batch', scatter_dimension=0, tiled=True)  176 us
    unnamed x1, blocking collectives  78.2 us
    unnamed x6, waiting for transfers between devices  59.9 us
    dot_general x3, matrix products, layer_backward(): jnp.einsum('rd,fd->rf', grad_ffn_low, w_out, preferred_element_type=jnp.f...  46.8 us
    dot_general x3, matrix products, layer_forward(): jnp.dot(normed_low, w_in, preferred_element_type=jnp.float32) + b_in  45 us
    reshape x21, local copies, waits for them, and re-layouts, head_split(): return rows.reshape(seq_count, length, HEADS, rows.shape[1] // HEADS)  43.3 us
    reduce_scatter x1, waiting for transfers between devices, per_device(): lax.psum_scatter(grad_totals[0], 'batch', scatter_dimension=0, tiled=True)  42.5 us
  transfers between devices with their start and end apart: 9, of which 4 were waited for; matrix products, arithmetic and copies ran while one was open for 17% of the time, Pallas kernels for 0%

commit v1 on v0

v1 whole, which is shorter than its diff:
```python
import functools
import math

import jax
import jax.numpy as jnp
from jax import lax
from jax.experimental import pallas as pl
from jax.experimental.pallas import tpu as pltpu
from jax.sharding import PartitionSpec as P

HEADS = 12
QLEN = 32
PLEN = 256


norm_eps = 1e-05


def normalize(inputs, gain_vec, shift_vec):
    mean_val = jnp.mean(inputs, -1, keepdims=True)
    centred = inputs - mean_val
    spread = jnp.mean(centred * centred, -1, keepdims=True)
    return centred * lax.rsqrt(spread + norm_eps) * gain_vec + shift_vec


def exact_gelu(inputs):
    return jax.nn.gelu(inputs, approximate=False)


def head_split(rows, seq_count, length):
    return rows.reshape(seq_count, length, HEADS, rows.shape[1] // HEADS)


def masked_scores(q_heads, k_heads, lengths, length):
    head_size = q_heads.shape[3]
    scores = jnp.einsum(
        "sqhd,skhd->shqk", q_heads, k_heads, preferred_element_type=jnp.float32
    ) * head_size ** (-0.5)
    valid_mask = jnp.arange(length)[None, :] < lengths[:, None]
    return jnp.where(valid_mask[:, None, None, :], scores, -1000000000.0)


def attend_forward(queries, key_rows, values, lengths, length):
    seq_count = lengths.shape[0]
    q_heads = head_split(queries, seq_count, length)
    k_heads = head_split(key_rows, seq_count, length)
    v_heads = head_split(values, seq_count, length)
    scores = masked_scores(q_heads, k_heads, lengths, length)
    top_score = jnp.max(scores, -1, keepdims=True)
    weights = jnp.exp(scores - top_score)
    total_sum = jnp.sum(weights, -1, keepdims=True)
    probs_low = (weights / total_sum).astype(jnp.bfloat16)
    mixed = jnp.einsum("shqk,skhd->sqhd", probs_low, v_heads, preferred_element_type=jnp.float32)
    return (mixed.reshape(queries.shape).astype(jnp.bfloat16), top_score + jnp.log(total_sum))


def attend_backward(queries, key_rows, values, lengths, length, log_sums, grad_mixed):
    seq_count = lengths.shape[0]
    q_heads = head_split(queries, seq_count, length)
    k_heads = head_split(key_rows, seq_count, length)
    v_heads = head_split(values, seq_count, length)
    head_scale = q_heads.shape[3] ** (-0.5)
    probs_full = jnp.exp(masked_scores(q_heads, k_heads, lengths, length) - log_sums)
    grad_heads = head_split(grad_mixed, seq_count, length)
    grad_probs = jnp.einsum(
        "sqhd,skhd->shqk", grad_heads, v_heads, preferred_element_type=jnp.float32
    )
    grad_values = jnp.einsum(
        "shqk,sqhd->skhd",
        probs_full.astype(jnp.bfloat16),
        grad_heads,
        preferred_element_type=jnp.float32,
    )
    inner_sum = jnp.sum(grad_probs * probs_full, -1, keepdims=True)
    grad_scores = (probs_full * (grad_probs - inner_sum)).astype(jnp.bfloat16)
    grad_queries = (
        jnp.einsum("shqk,skhd->sqhd", grad_scores, k_heads, preferred_element_type=jnp.float32)
        * head_scale
    )
    grad_keys = (
        jnp.einsum("shqk,sqhd->skhd", grad_scores, q_heads, preferred_element_type=jnp.float32)
        * head_scale
    )
    return tuple(
        (
            member.reshape(queries.shape).astype(jnp.bfloat16)
            for member in (grad_queries, grad_keys, grad_values)
        )
    )


def layer_forward(token_rows, query_lens, passage_lens, params):
    w_qkv, b_qv, w_o, b_o, g_attn, c_attn, w_in, b_in, w_out, b_out, g_ffn, c_ffn = params
    features = token_rows.shape[1]
    projected = jnp.dot(token_rows, w_qkv, preferred_element_type=jnp.float32)
    queries = (projected[:, :features] + b_qv[:features]).astype(jnp.bfloat16)
    key_rows = projected[:, features : 2 * features].astype(jnp.bfloat16)
    values = (projected[:, 2 * features :] + b_qv[features:]).astype(jnp.bfloat16)
    query_rows = query_lens.shape[0] * QLEN
    mixed_q, sums_q = attend_forward(
        queries[:query_rows], key_rows[:query_rows], values[:query_rows], query_lens, QLEN
    )
    mixed_p, sums_p = attend_forward(
        queries[query_rows:], key_rows[query_rows:], values[query_rows:], passage_lens, PLEN
    )
    mixed_rows = jnp.concatenate([mixed_q, mixed_p], 0)
    pre_attn = (
        token_rows.astype(jnp.float32)
        + jnp.dot(mixed_rows, w_o, preferred_element_type=jnp.float32)
        + b_o
    )
    normed = normalize(pre_attn, g_attn, c_attn)
    normed_low = normed.astype(jnp.bfloat16)
    up_proj = jnp.dot(normed_low, w_in, preferred_element_type=jnp.float32) + b_in
    act_low = exact_gelu(up_proj).astype(jnp.bfloat16)
    pre_ffn = normed + jnp.dot(act_low, w_out, preferred_element_type=jnp.float32) + b_out
    kept_state = (
        token_rows,
        queries,
        key_rows,
        values,
        mixed_rows,
        sums_q,
        sums_p,
        pre_attn,
        normed_low,
        up_proj,
        act_low,
        pre_ffn,
        query_lens,
        passage_lens,
    )
    return (normalize(pre_ffn, g_ffn, c_ffn), kept_state)


def layer_backward(kept_state, params, grad_out):
    (
        token_rows,
        queries,
        key_rows,
        values,
        mixed_rows,
        sums_q,
        sums_p,
        pre_attn,
        normed_low,
        up_proj,
        act_low,
        pre_ffn,
        query_lens,
        passage_lens,
    ) = kept_state
    w_qkv, b_qv, w_o, b_o, g_attn, c_attn, w_in, b_in, w_out, b_out, g_ffn, c_ffn = params
    unused, ffn_norm_back = jax.vjp(normalize, pre_ffn, g_ffn, c_ffn)
    grad_pre_ffn, grad_g_ffn, grad_c_ffn = ffn_norm_back(grad_out)
    grad_ffn_low = grad_pre_ffn.astype(jnp.bfloat16)
    grad_b_out = jnp.sum(grad_pre_ffn, 0)
    grad_act = jnp.einsum("rd,fd->rf", grad_ffn_low, w_out, preferred_element_type=jnp.float32)
    unused, gelu_back = jax.vjp(exact_gelu, up_proj)
    grad_up = gelu_back(grad_act)[0].astype(jnp.bfloat16)
    grad_b_in = jnp.sum(grad_up.astype(jnp.float32), 0)
    grad_normed = grad_pre_ffn + jnp.einsum(
        "rf,df->rd", grad_up, w_in, preferred_element_type=jnp.float32
    )
    unused, attn_norm_back = jax.vjp(normalize, pre_attn, g_attn, c_attn)
    grad_pre_attn, grad_g_attn, grad_c_attn = attn_norm_back(grad_normed)
    grad_attn_low = grad_pre_attn.astype(jnp.bfloat16)
    grad_b_o = jnp.sum(grad_pre_attn, 0)
    grad_mixed = jnp.einsum(
        "rd,ed->re", grad_attn_low, w_o, preferred_element_type=jnp.float32
    ).astype(jnp.bfloat16)
    query_rows = query_lens.shape[0] * QLEN
    grads_q = attend_backward(
        queries[:query_rows],
        key_rows[:query_rows],
        values[:query_rows],
        query_lens,
        QLEN,
        sums_q,
        grad_mixed[:query_rows],
    )
    grads_p = attend_backward(
        queries[query_rows:],
        key_rows[query_rows:],
        values[query_rows:],
        passage_lens,
        PLEN,
        sums_p,
        grad_mixed[query_rows:],
    )
    stacked = tuple((jnp.concatenate([left, right], 0) for left, right in zip(grads_q, grads_p)))
    grad_proj = jnp.concatenate(stacked, 1)
    grad_b_qv = jnp.concatenate(
        [jnp.sum(stacked[0].astype(jnp.float32), 0), jnp.sum(stacked[2].astype(jnp.float32), 0)]
    )
    grad_rows = grad_pre_attn + jnp.einsum(
        "re,de->rd", grad_proj, w_qkv, preferred_element_type=jnp.float32
    )
    lefts = (token_rows, mixed_rows, normed_low, act_low)
    rights = (grad_proj, grad_attn_low, grad_up, grad_ffn_low)
    vectors = (
        grad_b_qv,
        grad_b_o,
        grad_g_attn,
        grad_c_attn,
        grad_b_in,
        grad_b_out,
        grad_g_ffn,
        grad_c_ffn,
    )
    return (grad_rows, lefts, rights, vectors)


def contrast(logits, targets):
    top_score = jnp.max(logits, -1, keepdims=True)
    log_total = top_score[:, 0] + jnp.log(jnp.sum(jnp.exp(logits - top_score), -1))
    chosen = targets[:, None] == jnp.arange(logits.shape[1])[None, :]
    term_values = log_total - jnp.sum(jnp.where(chosen, logits, 0.0), -1)
    grad_logits = (jnp.exp(logits - log_total[:, None]) - chosen.astype(jnp.float32)).astype(
        jnp.bfloat16
    )
    return (term_values, grad_logits)


MESH = pl.DeviceIdType.MESH
CHUNK = 384
COUNT = 12
BLOCK = 48


def swap(value):
    return lax.ppermute(value, "section", [(0, 1), (1, 0)])


def chunk_left(ch):
    return (ch >= 3).astype(jnp.int32) + (ch >= 4).astype(jnp.int32) + jnp.maximum(ch - 7, 0)


def chunk_right(ch):
    return jnp.minimum(ch, 8)


def reduce_kernel(
    at1, pat1, g1, pg1, at0, pat0, g0, pg0, vec,
    o_qkv, o_o, o_in, o_out, o_vec,
    a_buf, g_buf, s1, r1, s2, r2, s3, r3, v1, w1, v2, w2, v3, w3,
    load, s1s, r1s, s2s, r2s, s3s, r3s, vs, vr, v3s, v3r,
):
    core = lax.axis_index("section")
    me = lax.axis_index("batch")
    x, y, z = me % 2, (me // 2) % 2, me // 4
    px, py = me + 1 - 2 * x, me + 2 - 4 * y

    loads = []
    for layer, parts in ((1, (at1, pat1, g1, pg1)), (0, (at0, pat0, g0, pg0))):
        for spot, part in enumerate(parts):
            lo = (spot % 2) * CHUNK
            if spot < 2:
                dst = a_buf.at[layer, :, :, :, pl.ds(lo, CHUNK)]
            else:
                dst = g_buf.at[layer, :, pl.ds(lo, CHUNK)]
            loads.append(pltpu.make_async_copy(part, dst, load.at[layer, spot]))
            loads[-1].start()
    vload = pltpu.make_async_copy(vec, v1, load.at[2, 0])
    vload.start()

    barrier = pltpu.get_barrier_semaphore()
    for who in (px, py):
        pl.semaphore_signal(barrier, inc=1, device_id={"batch": who}, device_id_type=MESH)
    for step in (1, 2, 3):
        other = ((z + step) % 4) * 4 + me % 4
        for sec in (0, 1):
            pl.semaphore_signal(
                barrier, inc=1, device_id={"section": sec, "batch": other}, device_id_type=MESH
            )
    pl.semaphore_signal(barrier, inc=1, device_id={"section": 1 - core}, device_id_type=MESH)
    pl.semaphore_wait(barrier, 9)

    def remote(src, dst, send, recv, where):
        return pltpu.make_async_remote_copy(
            src_ref=src, dst_ref=dst, send_sem=send, recv_sem=recv,
            device_id=where, device_id_type=MESH,
        )

    def first(k, par):
        return remote(
            s1.at[k % 4], r1.at[k], s1s.at[k], r1s.at[k], {"batch": px if par == 0 else py}
        )

    def second(k, par):
        return remote(
            s2.at[k % 4], r2.at[k], s2s.at[k], r2s.at[k], {"batch": py if par == 0 else px}
        )

    def third(k, step, src_core):
        layer = 1 - k // COUNT
        zt = (z + step) % 4
        return remote(
            s3.at[k % 4, zt],
            r3.at[src_core, k % COUNT, z],
            s3s.at[k, step],
            r3s.at[src_core, k % COUNT, z],
            {"section": layer, "batch": zt * 4 + me % 4},
        )

    def third_in(k, step, src_core):
        layer = 1 - k // COUNT
        zs = (z + 4 - step) % 4
        return remote(
            s3.at[k % 4, zs],
            r3.at[src_core, k % COUNT, zs],
            s3s.at[k, step],
            r3s.at[src_core, k % COUNT, zs],
            {"section": 1 - core, "batch": me},
        )

    def product(k, left, rows):
        ch, layer = k % COUNT, 1 - k // COUNT
        right = g_buf[layer, chunk_right(ch)]
        return jnp.dot(
            left.reshape(rows, 2 * CHUNK), right, preferred_element_type=jnp.float32
        )

    def left_of(k):
        return a_buf.at[1 - k // COUNT, chunk_left(k % COUNT)]

    def part_one(k, par):
        ref = left_of(k).reshape(4, 2, 2, BLOCK, 2 * CHUNK)
        left = ref[:, :, 1 - x] if par == 0 else ref[:, 1 - y]
        out = product(k, left, 8 * BLOCK)
        s1[k % 4] = out.astype(jnp.bfloat16).reshape(4, 2, BLOCK, CHUNK)
        first(k, par).start()

    def part_two(k, par):
        first(k, par).wait()
        ref = left_of(k).reshape(4, 2, 2, BLOCK, 2 * CHUNK)
        if par == 0:
            left, came = ref[:, 1 - y, x], r1[k, :, 1 - y]
        else:
            left, came = ref[:, y, 1 - x], r1[k, :, 1 - x]
        out = product(k, left, 4 * BLOCK).reshape(4, BLOCK, CHUNK) + came.astype(jnp.float32)
        s2[k % 4] = out.astype(jnp.bfloat16)
        second(k, par).start()

    def part_three(k, par):
        second(k, par).wait()
        layer = 1 - k // COUNT
        ref = left_of(k).reshape(4, 2, 2, BLOCK, 2 * CHUNK)
        came = r1[k, :, y] if par == 0 else r1[k, :, x]
        out = (
            product(k, ref[:, y, x], 4 * BLOCK).reshape(4, BLOCK, CHUNK)
            + came.astype(jnp.float32)
            + r2[k].astype(jnp.float32)
        )
        s3[k % 4] = out.astype(jnp.bfloat16)
        for step in (1, 2, 3):
            third(k, step, core).start()

        @pl.when(core != layer)
        def _():
            third(k, 0, core).start()

        @pl.when(core == layer)
        def _():
            r3[core, k % COUNT, z] = s3[k % 4, z]

    def part_four(k):
        layer = 1 - k // COUNT
        ch = k % COUNT
        for step in (1, 2, 3):
            third(k, step, core).wait_send()

        @pl.when(core != layer)
        def _():
            third(k, 0, core).wait_send()

        @pl.when(core == layer)
        def _():
            for step in (1, 2, 3):
                for src_core in (0, 1):
                    third_in(k, step, src_core).wait_recv()
            third_in(k, 0, 1 - core).wait_recv()
            for src_core in (0, 1):
                total = jnp.sum(r3[src_core, ch].astype(jnp.float32), 0)

                @pl.when(ch < 3)
                def _():
                    start = pl.multiple_of(ch * CHUNK + src_core * 1152, 128)
                    o_qkv[:, pl.ds(start, CHUNK)] = total

                @pl.when(ch == 3)
                def _():
                    o_o[:, pl.ds(src_core * CHUNK, CHUNK)] = total

                @pl.when((ch >= 4) & (ch < 8))
                def _():
                    start = pl.multiple_of((ch - 4) * CHUNK + src_core * 1536, 128)
                    o_in[:, pl.ds(start, CHUNK)] = total

                @pl.when(ch >= 8)
                def _():
                    o_out[ch - 8, :, pl.ds(src_core * CHUNK, CHUNK)] = total

    def vec_first():
        return remote(v2.at[0], w1, vs.at[0], vr.at[0], {"batch": px})

    def vec_second():
        return remote(v2.at[1, :, :, 0], w2, vs.at[1], vr.at[1], {"batch": py})

    def vec_third(layer, step):
        zt = (z + step) % 4
        return remote(
            v3.at[layer, zt], w3.at[core, z], v3s.at[layer, step], v3r.at[core, z],
            {"section": layer, "batch": zt * 4 + me % 4},
        )

    def vec_third_in(src_core, step):
        zs = (z + 4 - step) % 4
        return remote(
            v3.at[core, zs], w3.at[src_core, zs], v3s.at[core, step], v3r.at[src_core, zs],
            {"section": 1 - core, "batch": me},
        )

    for spot in range(4):
        loads[spot].wait()
    vload.wait()
    v2[0] = v1[:, :, :, 1 - x]
    vec_first().start()

    steps = 2 * COUNT + 6

    def pair(kk, carry):
        for par in (0, 1):
            k = 2 * kk + par

            @pl.when(k == COUNT)
            def _():
                for spot in range(4, 8):
                    loads[spot].wait()

            @pl.when(k < 2 * COUNT)
            def _():
                part_one(k, par)

            @pl.when((k >= 2) & (k < 2 * COUNT + 2))
            def _():
                part_two(k - 2, par)

            @pl.when((k >= 4) & (k < 2 * COUNT + 4))
            def _():
                part_three(k - 4, par)

            @pl.when(k >= 6)
            def _():
                part_four(k - 6)

        return carry

    lax.fori_loop(0, 3, pair, 0)
    vec_first().wait()
    v2[1, :, :, 0] = v1[:, :, 1 - y, x] + w1[:, :, 1 - y]
    vec_second().start()
    lax.fori_loop(3, 6, pair, 0)
    vec_second().wait()
    v3[...] = v1[:, :, y, x] + w1[:, :, y] + w2[...]
    for layer in (0, 1):
        for step in (1, 2, 3):
            vec_third(layer, step).start()

        @pl.when(core != layer)
        def _():
            vec_third(layer, 0).start()

        @pl.when(core == layer)
        def _():
            w3[core, z] = v3[layer, z]

    lax.fori_loop(6, steps // 2, pair, 0)
    for layer in (0, 1):
        for step in (1, 2, 3):
            vec_third(layer, step).wait_send()

        @pl.when(core != layer)
        def _():
            vec_third(layer, 0).wait_send()

    for step in (1, 2, 3):
        for src_core in (0, 1):
            vec_third_in(src_core, step).wait_recv()
    vec_third_in(1 - core, 0).wait_recv()
    o_vec[...] = jnp.sum(w3[...], (0, 1))


def reduce_all(packed, vec):
    low, full = jnp.bfloat16, jnp.float32
    steps = 2 * COUNT
    anywhere = pl.BlockSpec(memory_space=pl.ANY)
    vmem = pl.BlockSpec(memory_space=pltpu.VMEM)
    dma = pltpu.SemaphoreType.DMA
    return pl.pallas_call(
        reduce_kernel,
        out_shape=(
            jax.ShapeDtypeStruct((BLOCK, 2304), full),
            jax.ShapeDtypeStruct((BLOCK, 768), full),
            jax.ShapeDtypeStruct((BLOCK, 3072), full),
            jax.ShapeDtypeStruct((4, BLOCK, 768), full),
            jax.ShapeDtypeStruct((8, 128), full),
        ),
        in_specs=[anywhere] * 9,
        out_specs=(vmem,) * 5,
        scratch_shapes=[
            pltpu.VMEM((2, 7, 16, BLOCK, 2 * CHUNK), low),
            pltpu.VMEM((2, 9, 2 * CHUNK, CHUNK), low),
            pltpu.VMEM((4, 4, 2, BLOCK, CHUNK), low),
            pltpu.VMEM((steps, 4, 2, BLOCK, CHUNK), low),
            pltpu.VMEM((4, 4, BLOCK, CHUNK), low),
            pltpu.VMEM((steps, 4, BLOCK, CHUNK), low),
            pltpu.VMEM((4, 4, BLOCK, CHUNK), low),
            pltpu.VMEM((2, COUNT, 4, BLOCK, CHUNK), low),
            pltpu.VMEM((2, 4, 2, 2, 8, 128), full),
            pltpu.VMEM((2, 4, 2, 8, 128), full),
            pltpu.VMEM((2, 2, 4, 2, 8, 128), full),
            pltpu.VMEM((2, 4, 8, 128), full),
            pltpu.VMEM((2, 4, 8, 128), full),
            pltpu.VMEM((2, 4, 8, 128), full),
            dma((3, 4)),
            dma((steps,)),
            dma((steps,)),
            dma((steps,)),
            dma((steps,)),
            dma((steps, 4)),
            dma((2, COUNT, 4)),
            dma((2,)),
            dma((2,)),
            dma((2, 4)),
            dma((2, 4)),
        ],
        compiler_params=pltpu.CompilerParams(
            collective_id=1, has_side_effects=True, vmem_limit_bytes=56 * 1024 * 1024
        ),
    )(*packed, vec)


def pack_left(lefts):
    token_rows, mixed_rows, normed_low, act_low = (member.T for member in lefts)
    rows = token_rows.shape[1]
    shaped = [member.reshape(1, 16, BLOCK, rows) for member in (token_rows, mixed_rows, normed_low)]
    shaped.append(act_low.reshape(16, 4, BLOCK, rows).transpose(1, 0, 2, 3))
    return jnp.concatenate(shaped, 0)


def pack_right(rights, core):
    rows = rights[0].shape[0]
    parts = []
    for member in rights:
        width = member.shape[1] // 2
        half = lax.dynamic_slice_in_dim(member, core * width, width, 1)
        parts.append(half.reshape(rows, width // CHUNK, CHUNK).transpose(1, 0, 2))
    return jnp.concatenate(parts, 0)


def pack_vectors(vectors, parts):
    flat = jnp.concatenate([member.reshape(parts, -1) for member in vectors], 1)
    flat = jnp.pad(flat, ((0, 0), (0, 1024 - flat.shape[1])))
    return flat.reshape(parts, 8, 128)


def gather_kernel(parts, own, out, send, recv, here):
    core = lax.axis_index("section")
    me = lax.axis_index("batch")
    mine = core * parts + me
    total = 2 * parts
    barrier = pltpu.get_barrier_semaphore()

    def greet(step, carry):
        other = (mine + step) % total
        pl.semaphore_signal(
            barrier, inc=1, device_id={"section": other // parts, "batch": other % parts},
            device_id_type=MESH,
        )
        return carry

    lax.fori_loop(1, total, greet, 0)
    pl.semaphore_wait(barrier, total - 1)

    def copy(step, slot):
        other = (mine + step) % total
        return pltpu.make_async_remote_copy(
            src_ref=own, dst_ref=out.at[slot], send_sem=send.at[step], recv_sem=recv.at[slot],
            device_id={"section": other // parts, "batch": other % parts}, device_id_type=MESH,
        )

    def start(step, carry):
        copy(step, mine).start()
        return carry

    lax.fori_loop(1, total, start, 0)
    local = pltpu.make_async_copy(own, out.at[mine], here)
    local.start()
    local.wait()

    def finish(step, carry):
        copy(step, mine).wait_send()
        copy(step, (mine + total - step) % total).wait_recv()
        return carry

    lax.fori_loop(1, total, finish, 0)


def gather_all(own, parts):
    vmem = pl.BlockSpec(memory_space=pltpu.VMEM)
    return pl.pallas_call(
        functools.partial(gather_kernel, parts),
        out_shape=jax.ShapeDtypeStruct((2 * parts,) + own.shape, own.dtype),
        in_specs=[vmem],
        out_specs=vmem,
        scratch_shapes=[
            pltpu.SemaphoreType.DMA((2 * parts,)),
            pltpu.SemaphoreType.DMA((2 * parts,)),
            pltpu.SemaphoreType.DMA,
        ],
        compiler_params=pltpu.CompilerParams(collective_id=0, has_side_effects=True),
    )(own)


def per_device(
    parts,
    x_query,
    x_passage,
    len_query,
    len_passage,
    positive,
    cot_query,
    cot_passage,
    *weights,
):
    core = lax.axis_index("section")
    on_first = core == 0
    own_set = tuple(member[0] for member in weights)
    other_set = tuple(swap(member) for member in own_set)
    params = (
        tuple(jnp.where(on_first, a, b) for a, b in zip(own_set, other_set)),
        tuple(jnp.where(on_first, b, a) for a, b in zip(own_set, other_set)),
    )
    features = x_query.shape[2]
    half_q, half_p = x_query.shape[0] // 2, x_passage.shape[0] // 2
    split = half_q * QLEN

    def own_half(array):
        half = array.shape[0] // 2
        return lax.dynamic_slice_in_dim(array, core * half, half, 0)

    def rows_of(query, passage):
        return jnp.concatenate(
            [own_half(query).reshape(-1, features), own_half(passage).reshape(-1, features)], 0
        )

    query_lens, passage_lens = own_half(len_query), own_half(len_passage)
    out0, kept0 = layer_forward(rows_of(x_query, x_passage), query_lens, passage_lens, params[0])
    rows1 = out0.astype(jnp.bfloat16)
    out1, kept1 = layer_forward(rows1, query_lens, passage_lens, params[1])
    final = out1.astype(jnp.bfloat16)

    def join(first, second):
        mine = jnp.where(on_first, first, second)
        came = swap(jnp.where(on_first, second, first))
        low, high = jnp.where(on_first, mine, came), jnp.where(on_first, came, mine)
        query = jnp.concatenate([low[:split], high[:split]], 0)
        passage = jnp.concatenate([low[split:], high[split:]], 0)
        return query.reshape(x_query.shape)[None], passage.reshape(x_passage.shape)[None]

    hidden_q, hidden_p = join(rows1, final)

    cls_own = jnp.concatenate(
        [
            final[:split].reshape(half_q, QLEN, features)[:, 0],
            final[split:].reshape(half_p, PLEN, features)[:, 0],
        ],
        0,
    )
    targets = lax.all_gather(positive, "batch", axis=0, tiled=True)
    count = half_q + half_p
    if parts == 16:
        flat = jnp.pad(cls_own.reshape(-1, 128), ((0, 2), (0, 0)))
        every = gather_all(flat, parts)[:, : count * features // 128]
        every = every.reshape(2, parts, count, features)
    else:
        every = lax.all_gather(cls_own, ("section", "batch"), axis=0, tiled=True)
        every = every.reshape(2, parts, count, features)
    every = every.transpose(1, 0, 2, 3)
    cls_query = every[:, :, :half_q].reshape(-1, features)
    cls_passage = every[:, :, half_q:].reshape(-1, features)
    score_scale = 2.0 / math.sqrt(features)
    logits = (
        jnp.einsum("qd,pd->qp", cls_query, cls_passage, preferred_element_type=jnp.float32)
        * score_scale
    )
    term_values, grad_logits = contrast(logits, targets)
    loss_value = jnp.mean(term_values)
    mine = lax.axis_index("batch") * 2 + core
    own_logits = lax.dynamic_slice_in_dim(grad_logits, mine * half_q, half_q, 0)
    grad_cls_q = (
        jnp.einsum("qp,pd->qd", own_logits, cls_passage, preferred_element_type=jnp.float32)
        * score_scale
    )
    own_columns = lax.dynamic_slice_in_dim(grad_logits, mine * half_p, half_p, 1)
    grad_cls_p = (
        jnp.einsum("qp,qd->pd", own_columns, cls_query, preferred_element_type=jnp.float32)
        * score_scale
    )
    rows_list = []
    for cot, lens, cls_grad, length in (
        (cot_query, query_lens, grad_cls_q, QLEN),
        (cot_passage, passage_lens, grad_cls_p, PLEN),
    ):
        block = own_half(cot).astype(jnp.float32)
        valid_mask = jnp.arange(length)[None, :] < lens[:, None]
        masked = jnp.where(valid_mask[:, :, None], block, 0.0)
        rows_list.append(masked.at[:, 0].add(cls_grad).reshape(-1, features))
    grad_out1 = jnp.concatenate(rows_list, 0)

    grad1, lefts1, rights1, vectors1 = layer_backward(kept1, params[1], grad_out1)
    grad_low = grad1.astype(jnp.bfloat16).astype(jnp.float32)
    grad0, lefts0, rights0, vectors0 = layer_backward(kept0, params[0], grad_low)
    grad_q, grad_p = join(grad0, grad1)

    if parts == 16:
        packed = []
        for lefts, rights in ((lefts1, rights1), (lefts0, rights0)):
            left = pack_left(lefts)
            packed += [left, swap(left), pack_right(rights, core), swap(pack_right(rights, 1 - core))]
        vec = jnp.stack([pack_vectors(vectors0, parts), pack_vectors(vectors1, parts)])
        d_qkv, d_o, d_in, d_out, d_vec = reduce_all(packed, vec.reshape(2, 4, 2, 2, 8, 128))
        d_out = d_out.reshape(4 * BLOCK, 768)
        flat = d_vec.reshape(-1)
        sizes = [member.shape[0] // parts for member in vectors0]
        small, at = [], 0
        for size in sizes:
            small.append(flat[at : at + size])
            at += size
    else:

        def total(first, second):
            kept = jnp.where(on_first, first, second)
            both = kept + swap(jnp.where(on_first, second, first))
            return lax.psum_scatter(both, "batch", scatter_dimension=0, tiled=True)

        def product(left, right):
            return jnp.einsum("rd,re->de", left, right, preferred_element_type=jnp.float32)

        d_qkv, d_o, d_in, d_out = (
            total(product(la, ra), product(lb, rb))
            for la, ra, lb, rb in zip(lefts0, rights0, lefts1, rights1)
        )
        small = [total(first, second) for first, second in zip(vectors0, vectors1)]
    d_b_qv, d_b_o, d_g_attn, d_c_attn, d_b_in, d_b_out, d_g_ffn, d_c_ffn = small
    outs = (
        d_qkv, d_b_qv, d_o, d_b_o, d_g_attn, d_c_attn, d_in, d_b_in, d_out, d_b_out, d_g_ffn,
        d_c_ffn,
    )
    return (hidden_q, hidden_p, grad_q, grad_p, loss_value) + tuple(item[None] for item in outs)


def solution(mesh):
    in_specs = (
        P("batch", None, None),
        P("batch", None, None),
        P("batch"),
        P("batch"),
        P("batch"),
        P("batch", None, None),
        P("batch", None, None),
        P("section", None, None),
        P("section", None),
        P("section", None, None),
        P("section", None),
        P("section", None),
        P("section", None),
        P("section", None, None),
        P("section", None),
        P("section", None, None),
        P("section", None),
        P("section", None),
        P("section", None),
    )
    out_specs = (
        P("section", "batch", None, None),
        P("section", "batch", None, None),
        P("section", "batch", None, None),
        P("section", "batch", None, None),
        P(),
        P("section", "batch", None),
        P("section", "batch"),
        P("section", "batch", None),
        P("section", "batch"),
        P("section", "batch"),
        P("section", "batch"),
        P("section", "batch", None),
        P("section", "batch"),
        P("section", "batch", None),
        P("section", "batch"),
        P("section", "batch"),
        P("section", "batch"),
    )
    return jax.shard_map(
        functools.partial(per_device, mesh.shape["batch"]), mesh=mesh, in_specs=in_specs, out_specs=out_specs, check_vma=False
    )
```

time: 1230 us -> 579 us (0.47)
  waiting for transfers between devices: 455 us -> 0.05 us
  Pallas kernels: 0 us -> 153 us
  blocking collectives: 162 us -> 16.3 us
  matrix products: 270 us -> 154 us
  local copies, waits for them, and re-layouts: 217 us -> 155 us
  between operations: 26.3 us -> 5.83 us
    reduce_scatter x4 -> x0, waiting for transfers between devices: 395 us -> none  [the longest x1 177 us: per_device(): lax.psum_scatter(grad_totals[6], 'batch', scatter_dimension=0, tiled=True)]
    pallas_call x0 -> x2, Pallas kernels: none -> 153 us  [the longest x1 141 us: reduce_all(): pl.pallas_call(reduce_kernel, out_shape=(jax.ShapeDtypeStruct((BLOCK, 230...]
    unnamed x1, blocking collectives: 78.2 us -> 16.3 us
    dot_general x15 -> x3, matrix products: 63.4 us -> 3.27 us  [the longest x1 1.13 us: per_device(): jnp.einsum('qd,pd->qp', cls_query, cls_passage, preferred_element_type=jn...]
    unnamed x6 -> x0, waiting for transfers between devices: 59.9 us -> none
    all_gather x1 -> x0, blocking collectives: 42.3 us -> none  [per_device(): gathered = lax.all_gather(cls_passage, 'batch', axis=0, tiled=True)]
    psum x1 -> x0, blocking collectives: 41.8 us -> none  [per_device(): lax.psum(jnp.where(on_first, 0.0, jnp.sum(term_values)), ('section', 'bat...]
    reshape x21 -> x8, local copies, waits for them, and re-layouts: 43.3 us -> 9.56 us  [head_split(): return rows.reshape(seq_count, length, HEADS, rows.shape[1] // HEADS)]
  transfers between devices with their start and end apart: 9 -> 18, of which waited for: 4 -> 0; matrix products, arithmetic and copies ran while one was open for 17% -> 27% of each run, Pallas kernels for 0% -> 0%
where the time goes in v1:
time: 579 us; the launch traced here: 570 us
  local copies, waits for them, and re-layouts  155 us (27%)
  matrix products  154 us (27%)
  Pallas kernels  153 us (26%)
  other arithmetic  80 us (14%)
  blocking collectives  16.3 us (3%)
  between operations  5.83 us (1%)
    pallas_call x1, Pallas kernels, reduce_all(): pl.pallas_call(reduce_kernel, out_shape=(jax.ShapeDtypeStruct((BLOCK, 230...  141 us
    dot_general x2, matrix products, layer_backward(): jnp.einsum('rd,fd->rf', grad_ffn_low, w_out, preferred_element_type=jnp.f...  30.5 us
    dot_general x2, matrix products, layer_forward(): jnp.dot(normed_low, w_in, preferred_element_type=jnp.float32) + b_in  29 us
    dot_general x2, matrix products, layer_forward(): jnp.dot(act_low, w_out, preferred_element_type=jnp.float32)  28.9 us
    unnamed x406, local copies, waits for them, and re-layouts  24.8 us
    unnamed x1, blocking collectives  16.3 us
    reshape x8, local copies, waits for them, and re-layouts, pack_right(): parts.append(half.reshape(rows, width // CHUNK, CHUNK).transpose(1, 0, 2))  13.9 us
    convert_element_type x12, local copies, waits for them, and re-layouts, attend_backward(): member.reshape(queries.shape).astype(jnp.bfloat16)  13.9 us
  transfers between devices with their start and end apart: 18, of which 0 were waited for; matrix products, arithmetic and copies ran while one was open for 27% of the time, Pallas kernels for 0%

profile of v1, /device:TPU:0, one launch (start us, length us, event | category | flops | bytes accessed | tf_op | source)
XLA Modules:
  0.0 570.4 jit_solution(3876599553567091829)
XLA Ops:
  22.5 16.3 %all-reduce.3 = s32[128]{0:T(128)} all-reduce(s32[128]{0:T(128)S(1)} %dynamic-update-slice.7), channel_id=1, replica_groups=mesh['section'=2,'batch'=16] {'batch'}, use_global_device_ids=true, to_apply=%add.3 | all-reduce | flops 128 | bytes 1024
  49.5 2.6 fusion.193
  74.6 2.4 copy.178
  88.1 13.8 %fusion.7 = (bf16[3072,384]{0,1:T(8,128)(2,1)}, f32[384,3072]{1,0:T(8,128)S(1)}) fusion(f32[3072]{0:T(1024)S(1)} %copy-done.150, bf16[768,3072]{1,0:T(8,128)(2,1)} %collective-permute-done.6, pred[]{:T(512)S(6)} %eq.16, bf16[1,768,3072]{2,1,0:T(8,128)(2,1)S(1)} %bitcast.547, f32[384,768]{1,0:T(8,128)S(1)} %get-tuple-element.146, f32[768]{0:T(1024)S(1)} %copy-done.140, ...), kind=kOutput, calls=%fused_computation.11 | convolution fusion | flops 1893629952 | bytes 17716224 | tf_op jit(solution)/shard_map/dot_general | solution.py:114
  102.0 12.3 %fusion.197 = (f32[384]{0:T(512)S(1)}, f32[384,768]{1,0:T(8,128)S(1)}) fusion(f32[768]{0:T(1024)S(1)} %copy-done.169, bf16[3072,768]{1,0:T(8,128)(2,1)} %collective-permute-done.8, pred[]{:T(512)S(6)} %eq.16, bf16[1,3072,768]{2,1,0:T(8,128)(2,1)S(1)} %bitcast.540, f32[384,3072]{1,0:T(8,128)S(1)} %get-tuple-element.177, f32[3072]{0:T(1024)S(1)} %copy-done.150, ...), kind=kOutput, calls=%fused_computation.419 | convolution fusion | flops 1894219392 | bytes 16541185 | tf_op jit(solution)/shard_map/dot_general | solution.py:116
  116.3 3.7 fusion.198
  133.8 15.2 %fusion.4 = (bf16[3072,384]{0,1:T(8,128)(2,1)}, f32[384,3072]{1,0:T(8,128)S(1)}) fusion(f32[3072]{0:T(1024)S(1)} %copy-done.152, bf16[768,3072]{1,0:T(8,128)(2,1)} %collective-permute-done.6, pred[]{:T(512)S(6)} %eq.16, bf16[1,768,3072]{2,1,0:T(8,128)(2,1)S(1)} %bitcast.549, f32[384,768]{1,0:T(8,128)S(1)} %get-tuple-element.156, f32[768]{0:T(1024)S(1)} %copy-done.144, ...), kind=kOutput, calls=%fused_computation.8 | convolution fusion | flops 1893629952 | bytes 17716224 | tf_op jit(solution)/shard_map/dot_general | solution.py:114
  149.2 16.6 %fusion.202 = (f32[384]{0:T(512)S(1)}, f32[384,768]{1,0:T(8,128)S(1)}) fusion(f32[768]{0:T(1024)S(1)} %copy-done.167, bf16[3072,768]{1,0:T(8,128)(2,1)} %collective-permute-done.8, pred[]{:T(512)S(6)} %eq.16, bf16[1,3072,768]{2,1,0:T(8,128)(2,1)S(1)} %bitcast.542, f32[384,3072]{1,0:T(8,128)S(1)} %get-tuple-element.175, f32[3072]{0:T(1024)S(1)} %copy-done.152, ...), kind=kOutput, calls=%fused_computation.424 | convolution fusion | flops 1894219392 | bytes 16541185 | tf_op jit(solution)/shard_map/dot_general | solution.py:116
  172.2 12.5 %shard_map.314 = bf16[32,32,128]{2,1,0:T(8,128)(2,1)} custom-call(bf16[32,128]{1,0:T(8,128)(2,1)} %pad.15.own), custom_call_target="tpu_custom_call" | custom-call | tf_op jit(solution)/shard_map/pallas_call | solution.py:612
  206.2 2.6 multiply_reduce_fusion.2
  212.6 16.3 %convert_reduce_fusion = (f32[3072]{0:T(1024)}, bf16[384,3072]{1,0:T(8,128)(2,1)S(1)}) fusion(bf16[384,768]{1,0:T(8,128)(2,1)S(1)} %get-tuple-element.100, bf16[3072,768]{1,0:T(8,128)(2,1)} %collective-permute-done.8, pred[]{:T(512)S(6)} %eq.16, bf16[1,3072,768]{2,1,0:T(8,128)(2,1)} %param.38, f32[384,3072]{1,0:T(8,128)} %copy-done.180, ...), kind=kOutput, calls=%fused_computation.22 | convolution fusion | flops 1902769152 | bytes 17129472 | tf_op jit(solution)/shard_map/rd,fd->rf/dot_general | solution.py:158
  229.0 6.2 %multiply_reduce_fusion.3 = (f32[768]{0:T(1024)}, f32[384]{0:T(512)S(1)}, f32[768]{0:T(1024)}, f32[384,768]{1,0:T(8,128)S(1)}) fusion(f32[384,768]{1,0:T(8,128)S(1)} %copy-done.28, f32[384]{0:T(512)S(1)} %copy-done.157, f32[384]{0:T(512)S(1)} %copy-done.121, f32[768]{0:T(1024)S(1)} %copy-done.147, bf16[384,3072]{1,0:T(8,128)(2,1)S(1)} %get-tuple-element.179, ...), kind=kOutput, calls=%fused_computation.206 | convolution fusion | flops 1817245824 | bytes 15350785 | tf_op jit(solution)/shard_map/rf,df->rd/dot_general | solution.py:162
  260.6 2.5 copy.182
  266.3 2.6 maximum_maximum_fusion
  269.0 6.3 %fusion.112 = (f32[768]{0:T(1024)}, f32[384]{0:T(512)S(1)}, f32[768]{0:T(1024)}, bf16[384,768]{1,0:T(8,128)(2,1)S(1)}, f32[384,768]{1,0:T(8,128)}) fusion(f32[384,768]{1,0:T(8,128)S(1)} %copy-done.6, f32[384]{0:T(512)S(1)} %copy-done.113, f32[384]{0:T(512)S(1)} %copy-done.109, f32[768]{0:T(1024)S(1)} %copy-done.98, ...), kind=kOutput, calls=%fused_computation.195 | convolution fusion | flops 1374877824 | bytes 12991489 | tf_op jit(solution)/shard_map/re,de->rd/dot_general | solution.py:196
  276.7 14.2 %convert_reduce_fusion.1 = (f32[3072]{0:T(1024)}, bf16[384,3072]{1,0:T(8,128)(2,1)S(1)}) fusion(bf16[384,768]{1,0:T(8,128)(2,1)S(1)} %get-tuple-element.96, bf16[3072,768]{1,0:T(8,128)(2,1)} %collective-permute-done.8, pred[]{:T(512)S(6)} %eq.16, bf16[1,3072,768]{2,1,0:T(8,128)(2,1)S(1)} %bitcast.544, f32[384,3072]{1,0:T(8,128)S(1)} %bitcast.556, ...), kind=kOutput, calls=%fused_computation.23 | convolution fusion | flops 1902769152 | bytes 17129472 | tf_op jit(solution)/shard_map/rd,fd->rf/dot_general | solution.py:158
  290.9 3.3 multiply_reduce_fusion.4
  313.5 3.0 copy.158
  319.3 3.0 copy.148
  364.3 3.5 pad_maximum_fusion.1.at0
  383.5 5.3 broadcast_select_fusion.42
  398.5 2.5 copy.160
  404.8 2.9 pad_maximum_fusion.2.g1
  417.2 140.5 %shard_map.315 = (f32[48,2304]{1,0:T(8,128)}, f32[48,768]{1,0:T(8,128)}, f32[48,3072]{1,0:T(8,128)}, f32[4,48,768]{2,1,0:T(8,128)}, f32[8,128]{1,0:T(8,128)}) custom-call(bf16[7,16,48,384]{3,2,1,0:T(8,128)(2,1)} %pad_maximum_fusion.at1, bf16[7,16,48,384]{3,2,1,0:T(8,128)(2,1)} %collective-permute-done.14.pat1, bf16[9,384,384]{2,1,0:T(8,128)(2,1)} %pad_maximum_fusion.2.g1, ...), custom_call_target="tpu_custom_call" | custom-call | tf_op jit(solution)/shard_map/pallas_call | solution.py:500
  (698 shorter events, 254.3 us)
Async XLA Ops:
  0.7 48.8 %collective-permute-start = (bf16[768,2304]{1,0:T(8,128)(2,1)}, bf16[768,2304]{1,0:T(8,128)(2,1)}, u32[]{:S(2)}, u32[]{:S(2)}) collective-permute-start(bf16[768,2304]{1,0:T(8,128)(2,1)} %bitcast.449), channel_id=1, source_target_pairs={{0,16},{16,0},{1,17},{17,1},{2,18},{18,2},{3,19},{19,3},{4,20},{20... | collective-permute-start | bytes 10616840 | tf_op jit(solution)/shard_map/ppermute | solution.py:232
  1.9 36.9 %copy-start.139 = (f32[768]{0:T(1024)}, f32[768]{0:T(1024)S(1)}, u32[]{:S(2)}) copy-start(f32[768]{0:T(1024)S(1)} %reduce.25) | copy-start | bytes 9220
  1.9 36.9 %collective-permute-start.11 = (f32[768]{0:T(1024)S(1)}, f32[768]{0:T(1024)}, u32[]{:S(2)}, u32[]{:S(2)}) collective-permute-start(f32[768]{0:T(1024)S(1)} %reduce.25), channel_id=1, source_target_pairs={{0,16},{16,0},{1,17},{17,1},{2,18},{18,2},{3,19},{19,3},{4,20},{20... | collective-permute-start | bytes 9224 | tf_op jit(solution)/shard_map/ppermute | solution.py:232
  3.4 36.7 %collective-permute-start.10 = (f32[768]{0:T(1024)}, f32[768]{0:T(1024)}, u32[]{:S(2)}, u32[]{:S(2)}) collective-permute-start(f32[768]{0:T(1024)} %reduce.24), channel_id=1, source_target_pairs={{0,16},{16,0},{1,17},{17,1},{2,18},{18,2},{3,19},{19,3},{4,20},{20... | collective-permute-start | bytes 9224 | tf_op jit(solution)/shard_map/ppermute | solution.py:232
  5.1 36.9 %collective-permute-start.9 = (f32[768]{0:T(1024)}, f32[768]{0:T(1024)}, u32[]{:S(2)}, u32[]{:S(2)}) collective-permute-start(f32[768]{0:T(1024)} %reduce.23), channel_id=1, source_target_pairs={{0,16},{16,0},{1,17},{17,1},{2,18},{18,2},{3,19},{19,3},{4,20},{20... | collective-permute-start | bytes 9224 | tf_op jit(solution)/shard_map/ppermute | solution.py:232
  6.5 36.7 %collective-permute-start.5 = (f32[768]{0:T(1024)}, f32[768]{0:T(1024)}, u32[]{:S(2)}, u32[]{:S(2)}) collective-permute-start(f32[768]{0:T(1024)} %reduce.22), channel_id=1, source_target_pairs={{0,16},{16,0},{1,17},{17,1},{2,18},{18,2},{3,19},{19,3},{4,20},{20... | collective-permute-start | bytes 9224 | tf_op jit(solution)/shard_map/ppermute | solution.py:232
  11.8 37.7 %copy-start.9 = (bf16[1,768,2304]{2,1,0:T(8,128)(2,1)S(1)}, bf16[1,768,2304]{2,1,0:T(8,128)(2,1)}, u32[]{:S(2)}) copy-start(bf16[1,768,2304]{2,1,0:T(8,128)(2,1)} %param.30) | copy-start | bytes 10616836
  38.8 6.2 %collective-permute-start.4 = (f32[768]{0:T(1024)}, f32[768]{0:T(1024)S(1)}, u32[]{:S(2)}, u32[]{:S(2)}) collective-permute-start(f32[768]{0:T(1024)} %reduce.21), channel_id=1, source_target_pairs={{0,16},{16,0},{1,17},{17,1},{2,18},{18,2},{3,19},{19,3},{4,20},{20... | collective-permute-start | bytes 9224 | tf_op jit(solution)/shard_map/ppermute | solution.py:232
  40.1 76.2 %copy-start.104 = (f32[768]{0:T(1024)}, f32[768]{0:T(1024)S(1)}, u32[]{:S(2)}) copy-start(f32[768]{0:T(1024)S(1)} %get-tuple-element.130) | copy-start | bytes 9220
  40.1 6.2 %collective-permute-start.3 = (f32[768]{0:T(1024)}, f32[768]{0:T(1024)S(1)}, u32[]{:S(2)}, u32[]{:S(2)}) collective-permute-start(f32[768]{0:T(1024)} %reduce.20), channel_id=1, source_target_pairs={{0,16},{16,0},{1,17},{17,1},{2,18},{18,2},{3,19},{19,3},{4,20},{20... | collective-permute-start | bytes 9224 | tf_op jit(solution)/shard_map/ppermute | solution.py:232
  41.9 74.4 %copy-start.96 = (f32[768]{0:T(1024)}, f32[768]{0:T(1024)S(1)}, u32[]{:S(2)}) copy-start(f32[768]{0:T(1024)S(1)} %get-tuple-element.128) | copy-start | bytes 9220
  41.9 6.2 %collective-permute-start.1 = (f32[1536]{0:T(1024)S(1)}, f32[1536]{0:T(1024)S(1)}, u32[]{:S(2)}, u32[]{:S(2)}) collective-permute-start(f32[1536]{0:T(1024)S(1)} %reduce.19), channel_id=1, source_target_pairs={{0,16},{16,0},{1,17},{17,1},{2,18},{18,2},{3,19},{19,3},{4,20},{20... | collective-permute-start | bytes 18440 | tf_op jit(solution)/shard_map/ppermute | solution.py:232
  43.2 4.9 collective-permute-start.7
  45.0 38.0 %collective-permute-start.2 = (bf16[768,768]{1,0:T(8,128)(2,1)}, bf16[768,768]{1,0:T(8,128)(2,1)}, u32[]{:S(2)}, u32[]{:S(2)}) collective-permute-start(bf16[768,768]{1,0:T(8,128)(2,1)} %bitcast.554), channel_id=1, source_target_pairs={{0,16},{16,0},{1,17},{17,1},{2,18},{18,2},{3,19},{19,3},{4,20},{20... | collective-permute-start | bytes 3538952 | tf_op jit(solution)/shard_map/ppermute | solution.py:232
  46.3 55.6 %collective-permute-start.8 = (bf16[3072,768]{1,0:T(8,128)(2,1)}, bf16[3072,768]{1,0:T(8,128)(2,1)}, u32[]{:S(2)}, u32[]{:S(2)}) collective-permute-start(bf16[3072,768]{1,0:T(8,128)(2,1)} %bitcast.538), channel_id=1, source_target_pairs={{0,16},{16,0},{1,17},{17,1},{2,18},{18,2},{3,19},{19,3},{4,20},{20... | collective-permute-start | bytes 14155784 | tf_op jit(solution)/shard_map/ppermute | solution.py:232
  48.1 39.9 %collective-permute-start.6 = (bf16[768,3072]{1,0:T(8,128)(2,1)}, bf16[768,3072]{1,0:T(8,128)(2,1)}, u32[]{:S(2)}, u32[]{:S(2)}) collective-permute-start(bf16[768,3072]{1,0:T(8,128)(2,1)} %bitcast.545), channel_id=1, source_target_pairs={{0,16},{16,0},{1,17},{17,1},{2,18},{18,2},{3,19},{19,3},{4,20},{20... | collective-permute-start | bytes 14155784 | tf_op jit(solution)/shard_map/ppermute | solution.py:232
  166.7 33.1 %copy-start.32 = (f32[4,32,768]{2,0,1:T(4,128)S(1)}, f32[4,32,768]{2,0,1:T(4,128)}, u32[]{:S(2)}) copy-start(f32[4,32,768]{2,0,1:T(4,128)} %convert_select_fusion.1) | copy-start | bytes 1179652
  336.4 52.5 %collective-permute-start.12 = (bf16[384,768]{1,0:T(8,128)(2,1)}, bf16[384,768]{1,0:T(8,128)(2,1)}, u32[]{:S(2)}, u32[]{:S(2)}) collective-permute-start(bf16[384,768]{1,0:T(8,128)(2,1)} %get-tuple-element.75), channel_id=1, source_target_pairs={{0,16},{16,0},{1,17},{17,1},{2,18},{18,2},{3,19},{19,3},{4,20},{20... | collective-permute-start | bytes 1769480 | tf_op jit(solution)/shard_map/ppermute | solution.py:232
  367.8 49.4 %collective-permute-start.16 = (bf16[7,16,48,384]{3,2,1,0:T(8,128)(2,1)}, bf16[7,16,48,384]{3,2,1,0:T(8,128)(2,1)}, u32[]{:S(2)}, u32[]{:S(2)}) collective-permute-start(bf16[7,16,48,384]{3,2,1,0:T(8,128)(2,1)} %pad_maximum_fusion.1.at0), channel_id=1, source_target_pairs={{0,16},{16,0},{1,17},{17,1},{2,18},{18,2},{3,19},{19,3},{4,20},{20... | collective-permute-start | bytes 12386312 | tf_op jit(solution)/shard_map/ppermute | solution.py:232
  370.7 46.5 %collective-permute-start.14 = (bf16[7,16,48,384]{3,2,1,0:T(8,128)(2,1)}, bf16[7,16,48,384]{3,2,1,0:T(8,128)(2,1)}, u32[]{:S(2)}, u32[]{:S(2)}) collective-permute-start(bf16[7,16,48,384]{3,2,1,0:T(8,128)(2,1)} %pad_maximum_fusion.at1), channel_id=1, source_target_pairs={{0,16},{16,0},{1,17},{17,1},{2,18},{18,2},{3,19},{19,3},{4,20},{20... | collective-permute-start | bytes 12386312 | tf_op jit(solution)/shard_map/ppermute | solution.py:232
  374.0 43.2 %collective-permute-start.17 = (bf16[9,384,384]{2,1,0:T(8,128)(2,1)}, bf16[9,384,384]{2,1,0:T(8,128)(2,1)}, u32[]{:S(2)}, u32[]{:S(2)}) collective-permute-start(bf16[9,384,384]{2,1,0:T(8,128)(2,1)} %pad_maximum_fusion.5), channel_id=1, source_target_pairs={{0,16},{16,0},{1,17},{17,1},{2,18},{18,2},{3,19},{19,3},{4,20},{20... | collective-permute-start | bytes 7962632 | tf_op jit(solution)/shard_map/ppermute | solution.py:232
  377.8 39.4 %collective-permute-start.15 = (bf16[9,384,384]{2,1,0:T(8,128)(2,1)}, bf16[9,384,384]{2,1,0:T(8,128)(2,1)}, u32[]{:S(2)}, u32[]{:S(2)}) collective-permute-start(bf16[9,384,384]{2,1,0:T(8,128)(2,1)} %pad_maximum_fusion.3), channel_id=1, source_target_pairs={{0,16},{16,0},{1,17},{17,1},{2,18},{18,2},{3,19},{19,3},{4,20},{20... | collective-permute-start | bytes 7962632 | tf_op jit(solution)/shard_map/ppermute | solution.py:232
  388.9 24.4 %collective-permute-start.13 = (f32[384,768]{1,0:T(8,128)}, f32[384,768]{1,0:T(8,128)}, u32[]{:S(2)}, u32[]{:S(2)}) collective-permute-start(f32[384,768]{1,0:T(8,128)} %get-tuple-element.172), channel_id=1, source_target_pairs={{0,16},{16,0},{1,17},{17,1},{2,18},{18,2},{3,19},{19,3},{4,20},{20... | collective-permute-start | bytes 3538952 | tf_op jit(solution)/shard_map/ppermute | solution.py:232
  417.2 151.8 %copy-start.1 = (bf16[2,256,768]{2,1,0:T(8,128)(2,1)S(1)}, bf16[2,256,768]{2,1,0:T(8,128)(2,1)}, u32[]{:S(2)}) copy-start(bf16[2,256,768]{2,1,0:T(8,128)(2,1)} %param.24) | copy-start | bytes 2359300
  (191 other events, 1189.5 us)

commit v2 on v1

--- a/solution.py
+++ b/solution.py
@@ -14,201 +14,6 @@
 
 
 norm_eps = 1e-05
-
-
-def normalize(inputs, gain_vec, shift_vec):
-    mean_val = jnp.mean(inputs, -1, keepdims=True)
-    centred = inputs - mean_val
-    spread = jnp.mean(centred * centred, -1, keepdims=True)
-    return centred * lax.rsqrt(spread + norm_eps) * gain_vec + shift_vec
-
-
-def exact_gelu(inputs):
-    return jax.nn.gelu(inputs, approximate=False)
-
-
-def head_split(rows, seq_count, length):
-    return rows.reshape(seq_count, length, HEADS, rows.shape[1] // HEADS)
-
-
-def masked_scores(q_heads, k_heads, lengths, length):
-    head_size = q_heads.shape[3]
-    scores = jnp.einsum(
-        "sqhd,skhd->shqk", q_heads, k_heads, preferred_element_type=jnp.float32
-    ) * head_size ** (-0.5)
-    valid_mask = jnp.arange(length)[None, :] < lengths[:, None]
-    return jnp.where(valid_mask[:, None, None, :], scores, -1000000000.0)
-
-
-def attend_forward(queries, key_rows, values, lengths, length):
-    seq_count = lengths.shape[0]
-    q_heads = head_split(queries, seq_count, length)
-    k_heads = head_split(key_rows, seq_count, length)
-    v_heads = head_split(values, seq_count, length)
-    scores = masked_scores(q_heads, k_heads, lengths, length)
-    top_score = jnp.max(scores, -1, keepdims=True)
-    weights = jnp.exp(scores - top_score)
-    total_sum = jnp.sum(weights, -1, keepdims=True)
-    probs_low = (weights / total_sum).astype(jnp.bfloat16)
-    mixed = jnp.einsum("shqk,skhd->sqhd", probs_low, v_heads, preferred_element_type=jnp.float32)
-    return (mixed.reshape(queries.shape).astype(jnp.bfloat16), top_score + jnp.log(total_sum))
-
-
-def attend_backward(queries, key_rows, values, lengths, length, log_sums, grad_mixed):
-    seq_count = lengths.shape[0]
-    q_heads = head_split(queries, seq_count, length)
-    k_heads = head_split(key_rows, seq_count, length)
-    v_heads = head_split(values, seq_count, length)
-    head_scale = q_heads.shape[3] ** (-0.5)
-    probs_full = jnp.exp(masked_scores(q_heads, k_heads, lengths, length) - log_sums)
-    grad_heads = head_split(grad_mixed, seq_count, length)
-    grad_probs = jnp.einsum(
-        "sqhd,skhd->shqk", grad_heads, v_heads, preferred_element_type=jnp.float32
-    )
-    grad_values = jnp.einsum(
-        "shqk,sqhd->skhd",
-        probs_full.astype(jnp.bfloat16),
-        grad_heads,
-        preferred_element_type=jnp.float32,
-    )
-    inner_sum = jnp.sum(grad_probs * probs_full, -1, keepdims=True)
-    grad_scores = (probs_full * (grad_probs - inner_sum)).astype(jnp.bfloat16)
-    grad_queries = (
-        jnp.einsum("shqk,skhd->sqhd", grad_scores, k_heads, preferred_element_type=jnp.float32)
-        * head_scale
-    )
-    grad_keys = (
-        jnp.einsum("shqk,sqhd->skhd", grad_scores, q_heads, preferred_element_type=jnp.float32)
-        * head_scale
-    )
-    return tuple(
-        (
-            member.reshape(queries.shape).astype(jnp.bfloat16)
-            for member in (grad_queries, grad_keys, grad_values)
-        )
-    )
-
-
-def layer_forward(token_rows, query_lens, passage_lens, params):
-    w_qkv, b_qv, w_o, b_o, g_attn, c_attn, w_in, b_in, w_out, b_out, g_ffn, c_ffn = params
-    features = token_rows.shape[1]
-    projected = jnp.dot(token_rows, w_qkv, preferred_element_type=jnp.float32)
-    queries = (projected[:, :features] + b_qv[:features]).astype(jnp.bfloat16)
-    key_rows = projected[:, features : 2 * features].astype(jnp.bfloat16)
-    values = (projected[:, 2 * features :] + b_qv[features:]).astype(jnp.bfloat16)
-    query_rows = query_lens.shape[0] * QLEN
-    mixed_q, sums_q = attend_forward(
-        queries[:query_rows], key_rows[:query_rows], values[:query_rows], query_lens, QLEN
-    )
-    mixed_p, sums_p = attend_forward(
-        queries[query_rows:], key_rows[query_rows:], values[query_rows:], passage_lens, PLEN
-    )
-    mixed_rows = jnp.concatenate([mixed_q, mixed_p], 0)
-    pre_attn = (
-        token_rows.astype(jnp.float32)
-        + jnp.dot(mixed_rows, w_o, preferred_element_type=jnp.float32)
-        + b_o
-    )
-    normed = normalize(pre_attn, g_attn, c_attn)
-    normed_low = normed.astype(jnp.bfloat16)
-    up_proj = jnp.dot(normed_low, w_in, preferred_element_type=jnp.float32) + b_in
-    act_low = exact_gelu(up_proj).astype(jnp.bfloat16)
-    pre_ffn = normed + jnp.dot(act_low, w_out, preferred_element_type=jnp.float32) + b_out
-    kept_state = (
-        token_rows,
-        queries,
-        key_rows,
-        values,
-        mixed_rows,
-        sums_q,
-        sums_p,
-        pre_attn,
-        normed_low,
-        up_proj,
-        act_low,
-        pre_ffn,
-        query_lens,
-        passage_lens,
-    )
-    return (normalize(pre_ffn, g_ffn, c_ffn), kept_state)
-
-
-def layer_backward(kept_state, params, grad_out):
-    (
-        token_rows,
-        queries,
-        key_rows,
-        values,
-        mixed_rows,
-        sums_q,
-        sums_p,
-        pre_attn,
-        normed_low,
-        up_proj,
-        act_low,
-        pre_ffn,
-        query_lens,
-        passage_lens,
-    ) = kept_state
-    w_qkv, b_qv, w_o, b_o, g_attn, c_attn, w_in, b_in, w_out, b_out, g_ffn, c_ffn = params
-    unused, ffn_norm_back = jax.vjp(normalize, pre_ffn, g_ffn, c_ffn)
-    grad_pre_ffn, grad_g_ffn, grad_c_ffn = ffn_norm_back(grad_out)
-    grad_ffn_low = grad_pre_ffn.astype(jnp.bfloat16)
-    grad_b_out = jnp.sum(grad_pre_ffn, 0)
-    grad_act = jnp.einsum("rd,fd->rf", grad_ffn_low, w_out, preferred_element_type=jnp.float32)
-    unused, gelu_back = jax.vjp(exact_gelu, up_proj)
-    grad_up = gelu_back(grad_act)[0].astype(jnp.bfloat16)
-    grad_b_in = jnp.sum(grad_up.astype(jnp.float32), 0)
-    grad_normed = grad_pre_ffn + jnp.einsum(
-        "rf,df->rd", grad_up, w_in, preferred_element_type=jnp.float32
-    )
-    unused, attn_norm_back = jax.vjp(normalize, pre_attn, g_attn, c_attn)
-    grad_pre_attn, grad_g_attn, grad_c_attn = attn_norm_back(grad_normed)
-    grad_attn_low = grad_pre_attn.astype(jnp.bfloat16)
-    grad_b_o = jnp.sum(grad_pre_attn, 0)
-    grad_mixed = jnp.einsum(
-        "rd,ed->re", grad_attn_low, w_o, preferred_element_type=jnp.float32
-    ).astype(jnp.bfloat16)
-    query_rows = query_lens.shape[0] * QLEN
-    grads_q = attend_backward(
-        queries[:query_rows],
-        key_rows[:query_rows],
-        values[:query_rows],
-        query_lens,
-        QLEN,
-        sums_q,
-        grad_mixed[:query_rows],
-    )
-    grads_p = attend_backward(
-        queries[query_rows:],
-        key_rows[query_rows:],
-        values[query_rows:],
-        passage_lens,
-        PLEN,
-        sums_p,
-        grad_mixed[query_rows:],
-    )
-    stacked = tuple((jnp.concatenate([left, right], 0) for left, right in zip(grads_q, grads_p)))
-    grad_proj = jnp.concatenate(stacked, 1)
-    grad_b_qv = jnp.concatenate(
-        [jnp.sum(stacked[0].astype(jnp.float32), 0), jnp.sum(stacked[2].astype(jnp.float32), 0)]
-    )
-    grad_rows = grad_pre_attn + jnp.einsum(
-        "re,de->rd", grad_proj, w_qkv, preferred_element_type=jnp.float32
-    )
-    lefts = (token_rows, mixed_rows, normed_low, act_low)
-    rights = (grad_proj, grad_attn_low, grad_up, grad_ffn_low)
-    vectors = (
-        grad_b_qv,
-        grad_b_o,
-        grad_g_attn,
-        grad_c_attn,
-        grad_b_in,
-        grad_b_out,
-        grad_g_ffn,
-        grad_c_ffn,
-    )
-    return (grad_rows, lefts, rights, vectors)
 
 
 def contrast(logits, targets):
@@ -232,6 +37,469 @@
     return lax.ppermute(value, "section", [(0, 1), (1, 0)])
 
 
+LOW = jnp.bfloat16
+FULL = jnp.float32
+ROWS = 16
+TILE = 256
+LAST = (((1,), (1,)), ((), ()))
+FIRST = (((0,), (0,)), ((), ()))
+
+
+def dot(left, right):
+    return jnp.dot(left, right, preferred_element_type=FULL)
+
+
+def dot_last(left, right):
+    return lax.dot_general(left, right, LAST, preferred_element_type=FULL)
+
+
+def dot_first(left, right):
+    return lax.dot_general(left, right, FIRST, preferred_element_type=FULL)
+
+
+def over(count, body):
+    def step(index, carry):
+        body(index)
+        return carry
+
+    lax.fori_loop(0, count, step, 0)
+
+
+def row_range(index):
+    return pl.ds(pl.multiple_of(index * ROWS, ROWS), ROWS)
+
+
+def lane_range(index, width):
+    return pl.ds(pl.multiple_of(index * width, 128), width)
+
+
+def moments(block):
+    centred = block - jnp.mean(block, -1, keepdims=True)
+    spread = jnp.mean(centred * centred, -1, keepdims=True)
+    inverse = lax.rsqrt(spread + norm_eps)
+    return centred * inverse, inverse
+
+
+def gelu_pair(block):
+    size = jnp.abs(block)
+    t = 1.0 / (1.0 + (0.3275911 * math.sqrt(0.5)) * size)
+    bell = jnp.exp(-0.5 * block * block)
+    poly = 0.5 * 1.061405429
+    for term in (-1.453152027, 1.421413741, -0.284496736, 0.254829592):
+        poly = poly * t + 0.5 * term
+    tail = poly * t * bell
+    phi = jnp.where(block > 0, 1.0 - tail, tail)
+    return block * phi, phi + block * bell * (1.0 / math.sqrt(2.0 * math.pi))
+
+
+def head_lanes(rows, head):
+    lane = lax.broadcasted_iota(jnp.int32, (rows, 128), 1)
+    return (lane < 64) if head == 0 else (lane >= 64)
+
+
+def query_mask(lens, count):
+    rows = count * QLEN
+    row = lax.broadcasted_iota(jnp.int32, (rows, rows), 0)
+    column = lax.broadcasted_iota(jnp.int32, (rows, rows), 1)
+    limit = jnp.zeros((rows, rows), jnp.int32)
+    for item in range(count):
+        limit = jnp.where(column // QLEN == item, item * QLEN + lens[item], limit)
+    return (row // QLEN == column // QLEN) & (column < limit)
+
+
+def fetch_weights(core, layer, own, other, buffers, sem):
+    def copies(source):
+        return [
+            pltpu.make_async_copy(a, b, sem.at[spot])
+            for spot, (a, b) in enumerate(zip(source, buffers))
+        ]
+
+    @pl.when(core == layer)
+    def _():
+        for copy in copies(own):
+            copy.start()
+
+    @pl.when(core != layer)
+    def _():
+        for copy in copies(other):
+            copy.start()
+
+    return copies(own)
+
+
+def forward_kernel(
+    layer, x, qlens, plens, par, wqkv, wo, win, wout, xqkv, xo, xin, xout,
+    o_qkv, o_pq, o_pp, o_mixed, o_pre, o_normed, o_act, o_slope, o_ffn, o_out,
+    bqkv, bo, bin_, bout, qkv, pq, pp, mixed, pre, normed_full, normed, up, act, slope, ffn,
+    load, save,
+):
+    core = lax.axis_index("section")
+    features = x.shape[1]
+    total = x.shape[0]
+    count_q, count_p = qlens.shape[0], plens.shape[0]
+    split = count_q * QLEN
+    waits = fetch_weights(
+        core, layer, (wqkv, wo, win, wout), (xqkv, xo, xin, xout), (bqkv, bo, bin_, bout), load
+    )
+    saves = []
+
+    def keep(source, target):
+        saves.append(pltpu.make_async_copy(source, target, save.at[len(saves)]))
+        saves[-1].start()
+
+    waits[0].wait()
+
+    def project(tile):
+        lanes = lane_range(tile, TILE)
+        out = dot(x[...], bqkv[:, lanes])
+        third = features // TILE
+        bias_row = jnp.where(tile < third, par[0:1, lane_range(tile % third, TILE)], 0.0)
+        bias_row = jnp.where(tile >= 2 * third, par[1:2, lane_range(tile % third, TILE)], bias_row)
+        qkv[:, lanes] = (out + bias_row).astype(LOW)
+
+    over(3 * features // TILE, project)
+    keep(qkv, o_qkv)
+
+    def attend(lo, rows, mask, probs, base):
+        def pair(hp):
+            def part(offset):
+                return qkv[pl.ds(lo, rows), pl.ds(pl.multiple_of(offset + hp * 128, 128), 128)]
+
+            queries = part(0) * LOW(0.125)
+            keys, values = part(features), part(2 * features)
+            outs = []
+            for head in (0, 1):
+                masked = jnp.where(head_lanes(rows, head), queries, LOW(0))
+                scores = jnp.where(mask, dot_last(masked, keys), -1000000000.0)
+                weights = jnp.exp(scores - jnp.max(scores, -1, keepdims=True))
+                inverse = 1.0 / jnp.sum(weights, -1, keepdims=True)
+                low = (weights * inverse).astype(LOW)
+                probs[base + 2 * hp + head] = low
+                outs.append(dot(low, values))
+            both = jnp.where(head_lanes(rows, 0), outs[0], outs[1])
+            mixed[pl.ds(lo, rows), pl.ds(pl.multiple_of(hp * 128, 128), 128)] = both.astype(LOW)
+
+        over(features // 128, pair)
+
+    attend(0, split, query_mask(qlens, count_q), pq, 0)
+    for item in range(count_p):
+        column = lax.broadcasted_iota(jnp.int32, (PLEN, PLEN), 1)
+        attend(split + item * PLEN, PLEN, column < plens[item], pp, item * HEADS)
+    keep(pq, o_pq)
+    keep(pp, o_pp)
+    keep(mixed, o_mixed)
+
+    waits[1].wait()
+
+    def mix(tile):
+        lanes = lane_range(tile, TILE)
+        pre[:, lanes] = (
+            dot(mixed[...], bo[:, lanes]) + x[:, lanes].astype(FULL) + par[2:3, lanes]
+        )
+
+    over(features // TILE, mix)
+    keep(pre, o_pre)
+
+    def norm_one(index):
+        rows = row_range(index)
+        block = moments(pre[rows])[0] * par[3:4] + par[4:5]
+        normed_full[rows] = block
+        normed[rows] = block.astype(LOW)
+
+    over(total // ROWS, norm_one)
+    keep(normed, o_normed)
+    waits[2].wait()
+
+    def expand(tile):
+        lanes = lane_range(tile, features)
+        up[...] = dot(normed[...], bin_[:, lanes]) + par[pl.ds(5 + tile, 1)]
+
+        def bend(index):
+            rows = row_range(index)
+            value, steep = gelu_pair(up[rows])
+            act[rows, lanes] = value.astype(LOW)
+            slope[rows, lanes] = steep.astype(LOW)
+
+        over(total // ROWS, bend)
+
+    over(4, expand)
+    keep(act, o_act)
+    keep(slope, o_slope)
+    waits[3].wait()
+
+    def contract(tile):
+        lanes = lane_range(tile, TILE)
+        ffn[:, lanes] = dot(act[...], bout[:, lanes]) + normed_full[:, lanes] + par[9:10, lanes]
+
+    over(features // TILE, contract)
+    keep(ffn, o_ffn)
+
+    def norm_two(index):
+        rows = row_range(index)
+        o_out[rows] = (moments(ffn[rows])[0] * par[10:11] + par[11:12]).astype(LOW)
+
+    over(total // ROWS, norm_two)
+    for copy in saves:
+        copy.wait()
+
+
+VMEM_LIMIT = 56 * 1024 * 1024
+
+
+def forward_layer(layer, x, qlens, plens, par, own, other):
+    total, features = x.shape
+    wide = own[2].shape[1]
+    count_q, count_p = qlens.shape[0], plens.shape[0]
+    split = count_q * QLEN
+    kept = [
+        ((total, 3 * features), LOW),
+        ((HEADS, split, split), LOW),
+        ((HEADS * count_p, PLEN, PLEN), LOW),
+        ((total, features), LOW),
+        ((total, features), FULL),
+        ((total, features), LOW),
+        ((total, wide), LOW),
+        ((total, wide), LOW),
+        ((total, features), FULL),
+    ]
+    anywhere = pl.BlockSpec(memory_space=pl.ANY)
+    vmem = pl.BlockSpec(memory_space=pltpu.VMEM)
+    smem = pl.BlockSpec(memory_space=pltpu.SMEM)
+    buffers = [pltpu.VMEM(shape, kind) for shape, kind in kept]
+    buffers = (
+        buffers[:5]
+        + [pltpu.VMEM((total, features), FULL)]
+        + buffers[5:6]
+        + [pltpu.VMEM((total, features), FULL)]
+        + buffers[6:]
+    )
+    return pl.pallas_call(
+        functools.partial(forward_kernel, layer),
+        out_shape=[jax.ShapeDtypeStruct(shape, kind) for shape, kind in kept]
+        + [jax.ShapeDtypeStruct((total, features), LOW)],
+        in_specs=[vmem, smem, smem, vmem] + [anywhere] * 8,
+        out_specs=[anywhere] * 9 + [vmem],
+        scratch_shapes=[pltpu.VMEM(item.shape, item.dtype) for item in own]
+        + buffers
+        + [pltpu.SemaphoreType.DMA((4,)), pltpu.SemaphoreType.DMA((9,))],
+        compiler_params=pltpu.CompilerParams(vmem_limit_bytes=VMEM_LIMIT),
+    )(x, qlens, plens, par, *own, *other)
+
+
+def add_rows(block):
+    return jnp.sum(block.reshape(ROWS // 8, 8, block.shape[1]), 0)
+
+
+def norm_back(source, grad_of, gain, total, store):
+    features = source.shape[1]
+    zero = jnp.zeros((8, features), FULL)
+
+    def step(index, carry):
+        rows = row_range(index)
+        grad = grad_of(rows)
+        unit, inverse = moments(source[rows])
+        scaled = grad * gain
+        back = inverse * (
+            scaled
+            - jnp.mean(scaled, -1, keepdims=True)
+            - unit * jnp.mean(scaled * unit, -1, keepdims=True)
+        )
+        store(rows, back)
+        return (
+            carry[0] + add_rows(grad * unit),
+            carry[1] + add_rows(grad),
+            carry[2] + add_rows(back),
+        )
+
+    sums = lax.fori_loop(0, total // ROWS, step, (zero, zero, zero))
+    return [jnp.sum(item, 0, keepdims=True) for item in sums]
+
+
+def backward_kernel(
+    layer, grad, par, wqkv, wo, win, wout, xqkv, xo, xin, xout,
+    h_qkv, h_pq, h_pp, h_pre, h_slope, h_ffn,
+    o_proj, o_attn, o_up, o_flow, o_rows, o_par,
+    bqkv, bo, bin_, bout, qkv, pq, pp, pre, slope, ffn,
+    proj, attn_full, attn, steep, gup, flow_full, flow, gmixed,
+    load, fetch, save,
+):
+    core = lax.axis_index("section")
+    total, features = grad.shape
+    split = pq.shape[1]
+    count_p = pp.shape[0] // HEADS
+    gets = [
+        pltpu.make_async_copy(a, b, fetch.at[spot])
+        for spot, (a, b) in enumerate(
+            zip((h_ffn, h_slope, h_pre, h_qkv, h_pq, h_pp), (ffn, slope, pre, qkv, pq, pp))
+        )
+    ]
+    gets[0].start()
+    waits = fetch_weights(
+        core, layer, (wout, win, wo, wqkv), (xout, xin, xo, xqkv), (bout, bin_, bo, bqkv), load
+    )
+    for copy in gets[1:]:
+        copy.start()
+    saves = []
+
+    def keep(source, target):
+        saves.append(pltpu.make_async_copy(source, target, save.at[len(saves)]))
+        saves[-1].start()
+
+    gets[0].wait()
+
+    def store_ffn(rows, back):
+        flow_full[rows] = back
+        flow[rows] = back.astype(LOW)
+
+    gain, shift, bias = norm_back(ffn, lambda rows: grad[rows], par[10:11], total, store_ffn)
+    o_par[10:11], o_par[11:12], o_par[9:10] = gain, shift, bias
+    keep(flow, o_flow)
+    gets[1].wait()
+    waits[0].wait()
+
+    def shrink(tile):
+        lanes = lane_range(tile, features)
+        rows_of = pl.ds(pl.multiple_of(tile * features, 128), features)
+        steep[...] = dot_last(flow[...], bout[rows_of])
+
+        def bend(index, carry):
+            rows = row_range(index)
+            low = (steep[rows] * slope[rows, lanes].astype(FULL)).astype(LOW)
+            gup[rows, lanes] = low
+            return carry + add_rows(low.astype(FULL))
+
+        sums = lax.fori_loop(0, total // ROWS, bend, jnp.zeros((8, features), FULL))
+        o_par[pl.ds(5 + tile, 1)] = jnp.sum(sums, 0, keepdims=True)
+
+    over(4, shrink)
+    keep(gup, o_up)
+    waits[1].wait()
+
+    def widen(tile):
+        rows_of = pl.ds(pl.multiple_of(tile * TILE, TILE), TILE)
+        lanes = lane_range(tile, TILE)
+        flow_full[:, lanes] += dot_last(gup[...], bin_[rows_of])
+
+    over(features // TILE, widen)
+    gets[2].wait()
+
+    def store_attn(rows, back):
+        attn_full[rows] = back
+        attn[rows] = back.astype(LOW)
+
+    gain, shift, bias = norm_back(pre, lambda rows: flow_full[rows], par[3:4], total, store_attn)
+    o_par[3:4], o_par[4:5], o_par[2:3] = gain, shift, bias
+    keep(attn, o_attn)
+    waits[2].wait()
+
+    def unmix(tile):
+        rows_of = pl.ds(pl.multiple_of(tile * TILE, TILE), TILE)
+        gmixed[:, lane_range(tile, TILE)] = dot_last(attn[...], bo[rows_of]).astype(LOW)
+
+    over(features // TILE, unmix)
+    for copy in gets[3:]:
+        copy.wait()
+
+    def attend(lo, rows, probs, base):
+        def pair(hp):
+            def spot(offset):
+                return (
+                    pl.ds(lo, rows),
+                    pl.ds(pl.multiple_of(offset + hp * 128, 128), 128),
+                )
+
+            queries, keys, values = (qkv[spot(item * features)] for item in range(3))
+            back = gmixed[spot(0)]
+            parts = []
+            for head in (0, 1):
+                masked = jnp.where(head_lanes(rows, head), back, LOW(0))
+                low = probs[base + 2 * hp + head]
+                full = low.astype(FULL)
+                grad_probs = dot_last(masked, values)
+                inner = jnp.sum(grad_probs * full, -1, keepdims=True)
+                grad_scores = (full * (grad_probs - inner)).astype(LOW)
+                parts.append(
+                    (
+                        dot(grad_scores, keys) * 0.125,
+                        dot_first(grad_scores, queries) * 0.125,
+                        dot_first(low, back),
+                    )
+                )
+            first = head_lanes(rows, 0)
+            for item in range(3):
+                both = jnp.where(first, parts[0][item], parts[1][item])
+                proj[spot(item * features)] = both.astype(LOW)
+
+        over(features // 128, pair)
+
+    attend(0, split, pq, 0)
+    for item in range(count_p):
+        attend(split + item * PLEN, PLEN, pp, item * HEADS)
+    keep(proj, o_proj)
+
+    def bias_sums(index, carry):
+        rows = row_range(index)
+        return (
+            carry[0] + add_rows(proj[rows, pl.ds(0, features)].astype(FULL)),
+            carry[1] + add_rows(proj[rows, pl.ds(2 * features, features)].astype(FULL)),
+        )
+
+    zero = jnp.zeros((8, features), FULL)
+    sums = lax.fori_loop(0, total // ROWS, bias_sums, (zero, zero))
+    o_par[0:1] = jnp.sum(sums[0], 0, keepdims=True)
+    o_par[1:2] = jnp.sum(sums[1], 0, keepdims=True)
+    o_par[12:16] = jnp.zeros((4, features), FULL)
+    waits[3].wait()
+
+    def finish(tile):
+        rows_of = pl.ds(pl.multiple_of(tile * TILE, TILE), TILE)
+        lanes = lane_range(tile, TILE)
+        o_rows[:, lanes] = attn_full[:, lanes] + dot_last(proj[...], bqkv[rows_of])
+
+    over(features // TILE, finish)
+    for copy in saves:
+        copy.wait()
+
+
+def backward_layer(layer, grad, par, own, other, kept):
+    total, features = grad.shape
+    wide = own[2].shape[1]
+    h_qkv, h_pq, h_pp, h_mixed, h_pre, h_normed, h_act, h_slope, h_ffn = kept
+    held = (h_qkv, h_pq, h_pp, h_pre, h_slope, h_ffn)
+    anywhere = pl.BlockSpec(memory_space=pl.ANY)
+    vmem = pl.BlockSpec(memory_space=pltpu.VMEM)
+    shape = jax.ShapeDtypeStruct
+    scratch = [pltpu.VMEM(item.shape, item.dtype) for item in tuple(own) + held]
+    scratch += [
+        pltpu.VMEM((total, 3 * features), LOW),
+        pltpu.VMEM((total, features), FULL),
+        pltpu.VMEM((total, features), LOW),
+        pltpu.VMEM((total, features), FULL),
+        pltpu.VMEM((total, wide), LOW),
+        pltpu.VMEM((total, features), FULL),
+        pltpu.VMEM((total, features), LOW),
+        pltpu.VMEM((total, features), LOW),
+        pltpu.SemaphoreType.DMA((4,)),
+        pltpu.SemaphoreType.DMA((6,)),
+        pltpu.SemaphoreType.DMA((4,)),
+    ]
+    return pl.pallas_call(
+        functools.partial(backward_kernel, layer),
+        out_shape=[
+            shape((total, 3 * features), LOW),
+            shape((total, features), LOW),
+            shape((total, wide), LOW),
+            shape((total, features), LOW),
+            shape((total, features), FULL),
+            shape((16, features), FULL),
+        ],
+        in_specs=[vmem, vmem] + [anywhere] * 14,
+        out_specs=[anywhere] * 4 + [vmem] * 2,
+        scratch_shapes=scratch,
+        compiler_params=pltpu.CompilerParams(vmem_limit_bytes=VMEM_LIMIT),
+    )(grad, par, *own, *other, *held)
+
+
 def chunk_left(ch):
     return (ch >= 3).astype(jnp.int32) + (ch >= 4).astype(jnp.int32) + jnp.maximum(ch - 7, 0)
 
@@ -241,28 +509,97 @@
 
 
 def reduce_kernel(
-    at1, pat1, g1, pg1, at0, pat0, g0, pg0, vec,
-    o_qkv, o_o, o_in, o_out, o_vec,
-    a_buf, g_buf, s1, r1, s2, r2, s3, r3, v1, w1, v2, w2, v3, w3,
-    load, s1s, r1s, s2s, r2s, s3s, r3s, vs, vr, v3s, v3r,
+    tok1, mix1, nor1, act1, pro1, att1, gup1, flo1,
+    tok0, mix0, nor0, act0, pro0, att0, gup0, flo0, vec,
+    o_qkv, o_o, o_in, o_out, o_vec, land,
+    a_buf, g_buf, stage, s1, r1, s2, r2, s3, r3, v1, w1, v2, w2, v3, w3,
+    load, s1s, r1s, s2s, r2s, s3s, r3s, vs, vr, v3s, v3r, gl, gs, gr, ls, lr, sl,
 ):
     core = lax.axis_index("section")
     me = lax.axis_index("batch")
     x, y, z = me % 2, (me // 2) % 2, me // 4
     px, py = me + 1 - 2 * x, me + 2 - 4 * y
-
-    loads = []
-    for layer, parts in ((1, (at1, pat1, g1, pg1)), (0, (at0, pat0, g0, pg0))):
-        for spot, part in enumerate(parts):
-            lo = (spot % 2) * CHUNK
-            if spot < 2:
-                dst = a_buf.at[layer, :, :, :, pl.ds(lo, CHUNK)]
-            else:
-                dst = g_buf.at[layer, :, pl.ds(lo, CHUNK)]
-            loads.append(pltpu.make_async_copy(part, dst, load.at[layer, spot]))
-            loads[-1].start()
-    vload = pltpu.make_async_copy(vec, v1, load.at[2, 0])
+    rows = tok1.shape[0]
+    features = tok1.shape[1]
+
+    vload = pltpu.make_async_copy(vec, v1, load)
     vload.start()
+    groups, rights = [], []
+    for layer, lefts, grads in (
+        (1, (tok1, mix1, nor1, act1), (pro1, att1, gup1, flo1)),
+        (0, (tok0, mix0, nor0, act0), (pro0, att0, gup0, flo0)),
+    ):
+        for spot in range(7):
+            ref = lefts[min(spot, 3)]
+            lanes = pl.ds(max(spot - 3, 0) * features, features)
+            groups.append((layer, spot, ref.at[:, lanes]))
+        spot = 0
+        for ref in grads:
+            width = ref.shape[1] // 2
+            for item in range(width // CHUNK):
+                rights.append((layer, spot, ref, width, item))
+                spot += 1
+
+    def right_here(entry):
+        layer, spot, ref, width, item = entry
+        lanes = pl.ds(pl.multiple_of(core * width + item * CHUNK, 128), CHUNK)
+        return pltpu.make_async_copy(
+            ref.at[:, lanes], g_buf.at[layer, spot, pl.ds(0, rows)], gl.at[layer, spot]
+        )
+
+    def right_there(entry):
+        layer, spot, ref, width, item = entry
+        lanes = pl.ds(pl.multiple_of((1 - core) * width + item * CHUNK, 128), CHUNK)
+        return remote(
+            ref.at[:, lanes], g_buf.at[layer, spot, pl.ds(rows, rows)],
+            gs.at[layer, spot], gr.at[layer, spot], {"section": 1 - core},
+        )
+
+    def left_there(entry):
+        layer, spot, ref = entry
+        return remote(
+            ref, land.at[layer, spot], ls.at[layer, spot], lr.at[layer, spot],
+            {"section": 1 - core},
+        )
+
+    def stage_own(number):
+        layer, spot, ref = groups[number]
+        return pltpu.make_async_copy(ref, stage.at[number % 2, 0], sl.at[number % 2, 0])
+
+    def stage_peer(number):
+        layer, spot, ref = groups[number]
+        return pltpu.make_async_copy(
+            land.at[layer, spot], stage.at[number % 2, 1], sl.at[number % 2, 1]
+        )
+
+    def stage_start(number):
+        if number < len(groups):
+            stage_own(number).start()
+            left_there(groups[number]).wait_recv()
+            stage_peer(number).start()
+
+    def stage_wait(number):
+        stage_start(number + 1)
+        stage_own(number).wait()
+        stage_peer(number).wait()
+
+    def turn(number):
+        layer, spot, unused = groups[number]
+        stage_wait(number)
+        for side in (0, 1):
+            lanes = pl.ds(side * rows, rows)
+            for half in range(features // CHUNK):
+                block = stage[number % 2, side, :, pl.ds(half * CHUNK, CHUNK)].T
+                if spot < 3:
+                    a_buf[layer, spot, pl.ds(8 * half, 8), :, lanes] = block.reshape(
+                        8, BLOCK, rows
+                    )
+                else:
+                    shaped = block.reshape(2, 4, BLOCK, rows)
+                    for item in range(4):
+                        a_buf[
+                            layer, 3 + item, pl.ds(4 * (spot - 3) + 2 * half, 2), :, lanes
+                        ] = shaped[:, item]
 
     barrier = pltpu.get_barrier_semaphore()
     for who in (px, py):
@@ -324,7 +661,28 @@
     def left_of(k):
         return a_buf.at[1 - k // COUNT, chunk_left(k % COUNT)]
 
+    def ready(k, par):
+        layer, ch = 1 - k // COUNT, k % COUNT
+
+        @pl.when(ch <= 8)
+        def _():
+            mine = g_buf.at[layer, ch, pl.ds(0, rows)]
+            pltpu.make_async_copy(mine, mine, gl.at[layer, ch]).wait()
+            theirs = g_buf.at[layer, ch, pl.ds(rows, rows)]
+            remote(
+                theirs, theirs, gs.at[layer, ch], gr.at[layer, ch], {"section": 1 - core}
+            ).wait_recv()
+
+        for number, (owner, spot, unused) in enumerate(groups):
+            when = (1 - owner) * COUNT + (0, 3, 4, 8, 8, 8, 8)[spot]
+            if when % 2 == par:
+
+                @pl.when(k == when)
+                def _():
+                    turn(number)
+
     def part_one(k, par):
+        ready(k, par)
         ref = left_of(k).reshape(4, 2, 2, BLOCK, 2 * CHUNK)
         left = ref[:, :, 1 - x] if par == 0 else ref[:, 1 - y]
         out = product(k, left, 8 * BLOCK)
@@ -421,8 +779,16 @@
             {"section": 1 - core, "batch": me},
         )
 
-    for spot in range(4):
-        loads[spot].wait()
+    order = (0, 3, 4, 8, 8, 8, 8)
+    for entry in groups:
+        layer, spot = entry[:2]
+        for right in rights:
+            begin = right[1] == 0 if spot == 0 else order[spot - 1] < right[1] <= order[spot]
+            if right[0] == layer and begin:
+                right_here(right).start()
+                right_there(right).start()
+        left_there(entry).start()
+    stage_start(0)
     vload.wait()
     v2[0] = v1[:, :, :, 1 - x]
     vec_first().start()
@@ -432,11 +798,6 @@
     def pair(kk, carry):
         for par in (0, 1):
             k = 2 * kk + par
-
-            @pl.when(k == COUNT)
-            def _():
-                for spot in range(4, 8):
-                    loads[spot].wait()
 
             @pl.when(k < 2 * COUNT)
             def _():
@@ -489,6 +850,10 @@
             vec_third_in(src_core, step).wait_recv()
     vec_third_in(1 - core, 0).wait_recv()
     o_vec[...] = jnp.sum(w3[...], (0, 1))
+    for entry in rights:
+        right_there(entry).wait_send()
+    for entry in groups:
+        left_there(entry).wait_send()
 
 
 def reduce_all(packed, vec):
@@ -505,12 +870,14 @@
             jax.ShapeDtypeStruct((BLOCK, 3072), full),
             jax.ShapeDtypeStruct((4, BLOCK, 768), full),
             jax.ShapeDtypeStruct((8, 128), full),
+            jax.ShapeDtypeStruct((2, 7, CHUNK, 768), low),
         ),
-        in_specs=[anywhere] * 9,
-        out_specs=(vmem,) * 5,
+        in_specs=[anywhere] * 17,
+        out_specs=(vmem,) * 5 + (anywhere,),
         scratch_shapes=[
             pltpu.VMEM((2, 7, 16, BLOCK, 2 * CHUNK), low),
             pltpu.VMEM((2, 9, 2 * CHUNK, CHUNK), low),
+            pltpu.VMEM((2, 2, CHUNK, 768), low),
             pltpu.VMEM((4, 4, 2, BLOCK, CHUNK), low),
             pltpu.VMEM((steps, 4, 2, BLOCK, CHUNK), low),
             pltpu.VMEM((4, 4, BLOCK, CHUNK), low),
@@ -523,7 +890,7 @@
             pltpu.VMEM((2, 4, 8, 128), full),
             pltpu.VMEM((2, 4, 8, 128), full),
             pltpu.VMEM((2, 4, 8, 128), full),
-            dma((3, 4)),
+            dma,
             dma((steps,)),
             dma((steps,)),
             dma((steps,)),
@@ -534,6 +901,12 @@
             dma((2,)),
             dma((2, 4)),
             dma((2, 4)),
+            dma((2, 9)),
+            dma((2, 9)),
+            dma((2, 9)),
+            dma((2, 7)),
+            dma((2, 7)),
+            dma((2, 2)),
         ],
         compiler_params=pltpu.CompilerParams(
             collective_id=1, has_side_effects=True, vmem_limit_bytes=56 * 1024 * 1024
@@ -541,26 +914,9 @@
     )(*packed, vec)
 
 
-def pack_left(lefts):
-    token_rows, mixed_rows, normed_low, act_low = (member.T for member in lefts)
-    rows = token_rows.shape[1]
-    shaped = [member.reshape(1, 16, BLOCK, rows) for member in (token_rows, mixed_rows, normed_low)]
-    shaped.append(act_low.reshape(16, 4, BLOCK, rows).transpose(1, 0, 2, 3))
-    return jnp.concatenate(shaped, 0)
-
-
-def pack_right(rights, core):
-    rows = rights[0].shape[0]
-    parts = []
-    for member in rights:
-        width = member.shape[1] // 2
-        half = lax.dynamic_slice_in_dim(member, core * width, width, 1)
-        parts.append(half.reshape(rows, width // CHUNK, CHUNK).transpose(1, 0, 2))
-    return jnp.concatenate(parts, 0)
-
-
-def pack_vectors(vectors, parts):
-    flat = jnp.concatenate([member.reshape(parts, -1) for member in vectors], 1)
+def pack_vectors(par, parts):
+    rows = (par[0:2], par[2], par[3], par[4], par[5:9], par[9], par[10], par[11])
+    flat = jnp.concatenate([member.reshape(parts, -1) for member in rows], 1)
     flat = jnp.pad(flat, ((0, 0), (0, 1024 - flat.shape[1])))
     return flat.reshape(parts, 8, 128)
 
@@ -636,11 +992,15 @@
 ):
     core = lax.axis_index("section")
     on_first = core == 0
-    own_set = tuple(member[0] for member in weights)
-    other_set = tuple(swap(member) for member in own_set)
+    own_set = [member[0] for member in weights]
+    own = [own_set[item] for item in (0, 2, 6, 8)]
+    other = [swap(member) for member in own]
+    own_par = jnp.concatenate([own_set[item].reshape(-1) for item in (1, 3, 4, 5, 7, 9, 10, 11)])
+    own_par = jnp.pad(own_par, (0, 16 * 768 - own_par.shape[0])).reshape(16, 768)
+    other_par = swap(own_par)
     params = (
-        tuple(jnp.where(on_first, a, b) for a, b in zip(own_set, other_set)),
-        tuple(jnp.where(on_first, b, a) for a, b in zip(own_set, other_set)),
+        jnp.where(on_first, own_par, other_par),
+        jnp.where(on_first, other_par, own_par),
     )
     features = x_query.shape[2]
     half_q, half_p = x_query.shape[0] // 2, x_passage.shape[0] // 2
@@ -656,10 +1016,9 @@
         )
 
     query_lens, passage_lens = own_half(len_query), own_half(len_passage)
-    out0, kept0 = layer_forward(rows_of(x_query, x_passage), query_lens, passage_lens, params[0])
-    rows1 = out0.astype(jnp.bfloat16)
-    out1, kept1 = layer_forward(rows1, query_lens, passage_lens, params[1])
-    final = out1.astype(jnp.bfloat16)
+    rows0 = rows_of(x_query, x_passage)
+    *kept0, rows1 = forward_layer(0, rows0, query_lens, passage_lens, params[0], own, other)
+    *kept1, final = forward_layer(1, rows1, query_lens, passage_lens, params[1], own, other)
 
     def join(first, second):
         mine = jnp.where(on_first, first, second)
@@ -719,23 +1078,22 @@
         rows_list.append(masked.at[:, 0].add(cls_grad).reshape(-1, features))
     grad_out1 = jnp.concatenate(rows_list, 0)
 
-    grad1, lefts1, rights1, vectors1 = layer_backward(kept1, params[1], grad_out1)
+    *rights1, grad1, vectors1 = backward_layer(1, grad_out1, params[1], own, other, kept1)
     grad_low = grad1.astype(jnp.bfloat16).astype(jnp.float32)
-    grad0, lefts0, rights0, vectors0 = layer_backward(kept0, params[0], grad_low)
+    *rights0, grad0, vectors0 = backward_layer(0, grad_low, params[0], own, other, kept0)
+    lefts1 = (rows1, kept1[3], kept1[5], kept1[6])
+    lefts0 = (rows0, kept0[3], kept0[5], kept0[6])
     grad_q, grad_p = join(grad0, grad1)
 
     if parts == 16:
-        packed = []
-        for lefts, rights in ((lefts1, rights1), (lefts0, rights0)):
-            left = pack_left(lefts)
-            packed += [left, swap(left), pack_right(rights, core), swap(pack_right(rights, 1 - core))]
+        packed = [*lefts1, *rights1, *lefts0, *rights0]
         vec = jnp.stack([pack_vectors(vectors0, parts), pack_vectors(vectors1, parts)])
-        d_qkv, d_o, d_in, d_out, d_vec = reduce_all(packed, vec.reshape(2, 4, 2, 2, 8, 128))
+        d_qkv, d_o, d_in, d_out, d_vec, unused = reduce_all(packed, vec.reshape(2, 4, 2, 2, 8, 128))
         d_out = d_out.reshape(4 * BLOCK, 768)
         flat = d_vec.reshape(-1)
-        sizes = [member.shape[0] // parts for member in vectors0]
         small, at = [], 0
-        for size in sizes:
+        for count in (2, 1, 1, 1, 4, 1, 1, 1):
+            size = count * features // parts
             small.append(flat[at : at + size])
             at += size
     else:
@@ -752,7 +1110,18 @@
             total(product(la, ra), product(lb, rb))
             for la, ra, lb, rb in zip(lefts0, rights0, lefts1, rights1)
         )
-        small = [total(first, second) for first, second in zip(vectors0, vectors1)]
+        sums = [
+            (first.reshape(-1), second.reshape(-1))
+            for first, second in zip(jnp.split(vectors0, 16), jnp.split(vectors1, 16))
+        ]
+        groups = ((0, 1), (2,), (3,), (4,), (5, 6, 7, 8), (9,), (10,), (11,))
+        small = [
+            total(
+                jnp.concatenate([sums[item][0] for item in group]),
+                jnp.concatenate([sums[item][1] for item in group]),
+            )
+            for group in groups
+        ]
     d_b_qv, d_b_o, d_g_attn, d_c_attn, d_b_in, d_b_out, d_g_ffn, d_c_ffn = small
     outs = (
         d_qkv, d_b_qv, d_o, d_b_o, d_g_attn, d_c_attn, d_in, d_b_in, d_out, d_b_out, d_g_ffn,

time: 579 us -> 375 us (0.65)
  matrix products: 154 us -> 0.62 us
  Pallas kernels: 153 us -> 301 us
  local copies, waits for them, and re-layouts: 155 us -> 23.2 us
  other arithmetic: 80 us -> 19.4 us
    dot_general x40 -> x0, matrix products: 151 us -> none  [the longest x2 30.5 us: layer_backward(): jnp.einsum('rd,fd->rf', grad_ffn_low, w_out, preferred_element_type=jnp.f...]
    pallas_call x0 -> x4, Pallas kernels: none -> 149 us  [the longest x2 75.2 us: forward_layer(): pl.pallas_call(functools.partial(forward_kernel, layer), out_shape=[jax.S...]
    reshape x31 -> x5, local copies, waits for them, and re-layouts: 37.7 us -> 0.33 us  [the longest x4 0.32 us: pack_vectors(): flat = jnp.concatenate([member.reshape(parts, -1) for member in rows], 1)]
    convert_element_type x18 -> x0, local copies, waits for them, and re-layouts: 26.3 us -> none  [the longest x12 13.9 us: attend_backward(): member.reshape(queries.shape).astype(jnp.bfloat16)]
    reduce_sum x24 -> x0, other arithmetic: 19.4 us -> none  [the longest x4 5.43 us: normalize(): centred = inputs - mean_val]
    concatenate x12 -> x2, other arithmetic: 21.3 us -> 1.93 us  [the longest x1 1.07 us: per_device(): grad_out1 = jnp.concatenate(rows_list, 0)]
    unnamed x406 -> x55, local copies, waits for them, and re-layouts: 24.8 us -> 5.97 us
    slice x25 -> x6, local copies, waits for them, and re-layouts: 17.3 us -> 5.04 us  [the longest x2 1.86 us: pack_vectors(): par[11]]
  transfers between devices with their start and end apart: 18 -> 7, of which waited for: 0 -> 0; matrix products, arithmetic and copies ran while one was open for 27% -> 6% of each run, Pallas kernels for 0% -> 38%
where the time goes in v2:
time: 375 us; the launch traced here: 367 us
  Pallas kernels  301 us (80%)
  local copies, waits for them, and re-layouts  23.2 us (6%)
  other arithmetic  19.4 us (5%)
  blocking collectives  15.8 us (4%)
  between operations  3.98 us (1%)
    pallas_call x1, Pallas kernels, reduce_all(): pl.pallas_call(reduce_kernel, out_shape=(jax.ShapeDtypeStruct((BLOCK, 230...  140 us
    pallas_call x2, Pallas kernels, forward_layer(): pl.pallas_call(functools.partial(forward_kernel, layer), out_shape=[jax.S...  75.2 us
    pallas_call x2, Pallas kernels, backward_layer(): pl.pallas_call(functools.partial(backward_kernel, layer), out_shape=[shap...  73.3 us
    unnamed x1, blocking collectives  15.8 us
    pallas_call x1, Pallas kernels, gather_all(): pl.pallas_call(functools.partial(gather_kernel, parts), out_shape=jax.Sha...  12.5 us
  transfers between devices with their start and end apart: 7, of which 0 were waited for; matrix products, arithmetic and copies ran while one was open for 6% of the time, Pallas kernels for 38%

profile of v2, /device:TPU:0, one launch (start us, length us, event | category | flops | bytes accessed | tf_op | source)
XLA Modules:
  0.0 367.5 jit_solution(17631484994150905663)
XLA Ops:
  8.1 0.9 constant_dynamic-slice_fusion.2
  10.7 1.2 convert_select_fusion
  14.2 15.8 %all-reduce.4 = s32[128]{0:T(128)S(1)} all-reduce(s32[128]{0:T(128)S(1)} %dynamic-update-slice.7), channel_id=1, replica_groups=mesh['section'=2,'batch'=16] {'batch'}, use_global_device_ids=true, to_apply=%add.4 | all-reduce | flops 128 | bytes 1024
  30.7 1.0 copy-done.2
  31.7 37.6 %shard_map.314 = (bf16[384,2304]{1,0:T(8,128)(2,1)}, bf16[12,128,128]{2,1,0:T(8,128)(2,1)}, bf16[12,256,256]{2,1,0:T(8,128)(2,1)}, bf16[384,768]{1,0:T(8,128)(2,...) custom-call(bf16[384,768]{1,0:T(8,128)(2,1)} %pad_maximum_fusion.4.x, ...), custom_call_target="tpu_custom_call" | custom-call | tf_op jit(solution)/shard_map/pallas_call | solution.py:276
  69.3 37.6 %shard_map.315 = (bf16[384,2304]{1,0:T(8,128)(2,1)}, bf16[12,128,128]{2,1,0:T(8,128)(2,1)}, bf16[12,256,256]{2,1,0:T(8,128)(2,1)}, bf16[384,768]{1,0:T(8,128)(2,...) custom-call(bf16[384,768]{1,0:T(8,128)(2,1)} %get-tuple-element.78.x, ...), custom_call_target="tpu_custom_call" | custom-call | tf_op jit(solution)/shard_map/pallas_call | solution.py:276
  106.9 0.9 slice.166
  107.9 1.0 slice_bitcast_fusion
  109.6 12.5 %shard_map.316 = bf16[32,32,128]{2,1,0:T(8,128)(2,1)} custom-call(bf16[32,128]{1,0:T(8,128)(2,1)} %pad.20.own), custom_call_target="tpu_custom_call" | custom-call | tf_op jit(solution)/shard_map/pallas_call | solution.py:968
  122.1 1.2 reshape.206
  125.8 1.1 pad_maximum_fusion.1.grad
  126.8 36.7 %shard_map.317 = (bf16[384,2304]{1,0:T(8,128)(2,1)}, bf16[384,768]{1,0:T(8,128)(2,1)}, bf16[384,3072]{1,0:T(8,128)(2,1)}, bf16[384,768]{1,0:T(8,128)(2,1)}, f32[384,768]{1,0:T(8,128)}, /*index=5*/f32[16,768]{1,0:T(8,128)}) custom-call(f32[384,768]{1,0:T(8,128)} %pad_maximum_fusion.1.grad, f32[16,768]{1,0:T(8,128)} %get-tuple-element.137.par, ...), custom_call_target="tpu_custom_call" | custom-call | tf_op jit(solution)/shard_map/pallas_call | solution.py:486
  167.0 1.1 convert_convert_fusion.grad
  168.1 36.6 %shard_map.318 = (bf16[384,2304]{1,0:T(8,128)(2,1)}, bf16[384,768]{1,0:T(8,128)(2,1)}, bf16[384,3072]{1,0:T(8,128)(2,1)}, bf16[384,768]{1,0:T(8,128)(2,1)}, f32[384,768]{1,0:T(8,128)}, /*index=5*/f32[16,768]{1,0:T(8,128)}) custom-call(f32[384,768]{1,0:T(8,128)} %convert_convert_fusion.grad, f32[16,768]{1,0:T(8,128)} %get-tuple-element.138.par, ...), custom_call_target="tpu_custom_call" | custom-call | tf_op jit(solution)/shard_map/pallas_call | solution.py:486
  206.2 0.9 slice_reduce_fusion.6
  208.6 1.2 broadcast_select_fusion.2
  209.8 1.8 collective-permute-start.6
  212.4 140.1 %shard_map.319 = (f32[48,2304]{1,0:T(8,128)}, f32[48,768]{1,0:T(8,128)}, f32[48,3072]{1,0:T(8,128)}, f32[4,48,768]{2,1,0:T(8,128)}, f32[8,128]{1,0:T(8,128)}, /*index=5*/bf16[2,7,384,768]{3,2,1,0:T(8,128)(2,1)}) custom-call(bf16[384,768]{1,0:T(8,128)(2,1)} %get-tuple-element.78.x.tok1, bf16[384,768]{1,0:T(8,128)(2,1)} %get-tuple-element.94.mix1, ...), custom_call_target="tpu_custom_call" | custom-call | tf_op jit(solution)/shard_map/pallas_call | solution.py:865
  352.4 1.3 slice.198
  354.4 1.2 slice_bitcast_fusion.8
  355.6 1.5 slice_bitcast_fusion.2
  357.1 1.2 broadcast_select_fusion.5
  359.1 0.9 pad_maximum_fusion.2
  360.6 1.2 pad_maximum_fusion
  (144 shorter events, 27.0 us)
Async XLA Ops:
  0.7 8.4 %copy-start = (bf16[2,256,768]{2,1,0:T(8,128)(2,1)S(1)}, bf16[2,256,768]{2,1,0:T(8,128)(2,1)}, u32[]{:S(2)}) copy-start(bf16[2,256,768]{2,1,0:T(8,128)(2,1)} %param.24) | copy-start | bytes 2359300
  0.7 8.4 %copy-start.12 = (bf16[8,32,768]{2,1,0:T(8,128)(2,1)S(1)}, bf16[8,32,768]{2,1,0:T(8,128)(2,1)}, u32[]{:S(2)}) copy-start(bf16[8,32,768]{2,1,0:T(8,128)(2,1)} %param.28) | copy-start | bytes 1179652
  0.7 8.4 %copy-start.14 = (s32[2]{0:T(128)S(1)}, s32[2]{0:T(128)}, u32[]{:S(2)}) copy-start(s32[2]{0:T(128)} %param.26) | copy-start | bytes 28
  0.7 9.0 %copy-start.15 = (s32[8]{0:T(128)S(1)}, s32[8]{0:T(128)}, u32[]{:S(2)}) copy-start(s32[8]{0:T(128)} %param.25) | copy-start | bytes 100
  0.7 30.0 %collective-permute-start.3 = (bf16[768,3072]{1,0:T(8,128)(2,1)}, bf16[768,3072]{1,0:T(8,128)(2,1)}, u32[]{:S(2)}, u32[]{:S(2)}) collective-permute-start(bf16[768,3072]{1,0:T(8,128)(2,1)} %bitcast.70), channel_id=1, source_target_pairs={{0,16},{16,0},{1,17},{17,1},{2,18},{18,2},{3,19},{19,3},{4,20},{20... | collective-permute-start | bytes 14155784 | tf_op jit(solution)/shard_map/ppermute | solution.py:37
  1.2 29.5 %collective-permute-start.4 = (bf16[3072,768]{1,0:T(8,128)(2,1)}, bf16[3072,768]{1,0:T(8,128)(2,1)}, u32[]{:S(2)}, u32[]{:S(2)}) collective-permute-start(bf16[3072,768]{1,0:T(8,128)(2,1)} %bitcast.75), channel_id=1, source_target_pairs={{0,16},{16,0},{1,17},{17,1},{2,18},{18,2},{3,19},{19,3},{4,20},{20... | collective-permute-start | bytes 14155784 | tf_op jit(solution)/shard_map/ppermute | solution.py:37
  1.3 29.4 %collective-permute-start.1 = (bf16[768,2304]{1,0:T(8,128)(2,1)}, bf16[768,2304]{1,0:T(8,128)(2,1)}, u32[]{:S(2)}, u32[]{:S(2)}) collective-permute-start(bf16[768,2304]{1,0:T(8,128)(2,1)} %bitcast.80), channel_id=1, source_target_pairs={{0,16},{16,0},{1,17},{17,1},{2,18},{18,2},{3,19},{19,3},{4,20},{20... | collective-permute-start | bytes 10616840 | tf_op jit(solution)/shard_map/ppermute | solution.py:37
  7.5 22.5 %collective-permute-start = (f32[16,768]{1,0:T(8,128)S(1)}, f32[16,768]{1,0:T(8,128)S(1)}, u32[]{:S(2)}, u32[]{:S(2)}) collective-permute-start(f32[16,768]{1,0:T(8,128)S(1)} %reshape.202), channel_id=1, source_target_pairs={{0,16},{16,0},{1,17},{17,1},{2,18},{18,2},{3,19},{19,3},{4,20},{20... | collective-permute-start | bytes 147464 | tf_op jit(solution)/shard_map/ppermute | solution.py:37
  7.6 23.0 %collective-permute-start.2 = (bf16[768,768]{1,0:T(8,128)(2,1)}, bf16[768,768]{1,0:T(8,128)(2,1)S(1)}, u32[]{:S(2)}, u32[]{:S(2)}) collective-permute-start(bf16[768,768]{1,0:T(8,128)(2,1)} %bitcast.85), channel_id=1, source_target_pairs={{0,16},{16,0},{1,17},{17,1},{2,18},{18,2},{3,19},{19,3},{4,20},{20... | collective-permute-start | bytes 3538952 | tf_op jit(solution)/shard_map/ppermute | solution.py:37
  9.8 2.1 copy-start.13
  10.6 2.1 copy-start.17
  10.7 3.3 copy-start.16
  126.8 39.3 %copy-start.4 = (bf16[384,768]{1,0:T(8,128)(2,1)S(1)}, bf16[384,768]{1,0:T(8,128)(2,1)}, u32[]{:S(2)}) copy-start(bf16[384,768]{1,0:T(8,128)(2,1)} %get-tuple-element.78.x.tok1) | copy-start | bytes 1769476
  126.8 39.3 %copy-start.6 = (bf16[384,768]{1,0:T(8,128)(2,1)S(1)}, bf16[384,768]{1,0:T(8,128)(2,1)}, u32[]{:S(2)}) copy-start(bf16[384,768]{1,0:T(8,128)(2,1)} %get-tuple-element.79) | copy-start | bytes 1769476
  163.5 3.5 copy-start.3
  207.9 149.1 %collective-permute-start.5 = (bf16[384,768]{1,0:T(8,128)(2,1)}, bf16[384,768]{1,0:T(8,128)(2,1)}, u32[]{:S(2)}, u32[]{:S(2)}) collective-permute-start(bf16[384,768]{1,0:T(8,128)(2,1)} %broadcast_select_fusion.6), channel_id=1, source_target_pairs={{0,16},{16,0},{1,17},{17,1},{2,18},{18,2},{3,19},{19,3},{4,20},{20... | collective-permute-start | bytes 1769480 | tf_op jit(solution)/shard_map/ppermute | solution.py:37
  209.8 150.3 %collective-permute-start.6 = (f32[384,768]{1,0:T(8,128)}, f32[384,768]{1,0:T(8,128)S(1)}, u32[]{:S(2)}, u32[]{:S(2)}) collective-permute-start(f32[384,768]{1,0:T(8,128)} %broadcast_select_fusion.2), channel_id=1, source_target_pairs={{0,16},{16,0},{1,17},{17,1},{2,18},{18,2},{3,19},{19,3},{4,20},{20... | collective-permute-start | bytes 3538952 | tf_op jit(solution)/shard_map/ppermute | solution.py:37
  212.4 144.7 %copy-start.5 = (bf16[384,768]{1,0:T(8,128)(2,1)S(1)}, bf16[384,768]{1,0:T(8,128)(2,1)}, u32[]{:S(2)}) copy-start(bf16[384,768]{1,0:T(8,128)(2,1)} %get-tuple-element.78.x.tok1) | copy-start | bytes 1769476
  358.3 1.7 copy-start.7
  361.8 1.2 copy-start.10
  361.8 1.9 copy-start.11
  361.8 2.6 copy-start.9
  363.0 2.3 copy-start.8
  363.8 2.3 copy-start.1
  (1 other events, 1.0 us)
